TPU v7x, 32 devices: a whole 2x2x4 slice. The times are simulated.
32 devices in a mesh: seq: 8 (over z, x), head: 4 (over y, core).
Axes of the slice: x: 2, y: 2, z: 4, core: 2. Of those that a mesh axis runs over, the one named last changes fastest.
Arguments:
- tokens: bfloat16 [2048, 1024], P('seq'), may hold values from -6 to 6
- attn_gain: bfloat16 [1024], replicated, may hold values from 0.099609375 to 1.8984375
- w_in: bfloat16 [1024, 3072], P(None, 'head'), may hold values from -0.1875 to 0.1875
- conv_weight: bfloat16 [4, 2048], P(None, 'head'), may hold values from -3 to 3
- gate_down: bfloat16 [1024, 16], replicated, may hold values from -0.1875 to 0.1875
- gate_up: bfloat16 [16, 512], P(None, 'head'), may hold values from -1.5 to 1.5
- forget_bias: bfloat16 [512], P('head'), may hold values from 0.5 to 10
- out_gain: bfloat16 [256], replicated, may hold values from 0.099609375 to 1.8984375
- w_out: bfloat16 [1024, 1024], P('head'), may hold values from -0.375 to 0.375
- mlp_gain: bfloat16 [1024], replicated, may hold values from 0.099609375 to 1.8984375
- w_gate_up: bfloat16 [1024, 5632], P(None, 'head'), may hold values from -0.1875 to 0.1875
- w_down: bfloat16 [2816, 1024], P('head'), may hold values from -0.21875 to 0.21875
- cotangent: bfloat16 [2048, 1024], P('seq'), may hold values from -6 to 6
Outputs:
- block_out: bfloat16 [2048, 1024], P('seq')
- grad_tokens: bfloat16 [2048, 1024], P('seq')
- grad_attn_gain: float32 [1024], P('seq')
- grad_w_in: float32 [1024, 3072], P('seq', 'head')
- grad_conv_weight: float32 [4, 2048], P(None, 'head')
- grad_gate_down: float32 [1024, 16], P('seq')
- grad_gate_up: float32 [16, 512], P(None, 'head')
- grad_forget_bias: float32 [512], P('head')
- grad_out_gain: float32 [256], replicated
- grad_w_out: float32 [1024, 1024], P('head', 'seq')
- grad_mlp_gain: float32 [1024], P('seq')
- grad_w_gate_up: float32 [1024, 5632], P('seq', 'head')
- grad_w_down: float32 [2816, 1024], P('head', 'seq')
All inputs are finite; a program needn't handle non-finite values.
Results may differ from a plain program's by a relative error of at most 0.02.
The roundings to bfloat16 on the way count: a program that leaves them out, or rounds other values in their place, can miss the bound.
Values may be sent and summed in bfloat16 or wider, within the bound.
A program may use at most 128 MiB of HBM per device.

v0:
```python
import jax
import jax.numpy as jnp
from jax import lax
from jax.sharding import PartitionSpec as P

SPAN = 64


norm_eps = 1e-05


def from_behind(value, axis, steps):
    count = lax.axis_size(axis)
    leading, last = (max(0, -steps), min(count, count - steps))
    return lax.ppermute(value, axis, [(source, source + steps) for source in range(leading, last)])


def prefix_2(value, axis, join, neutral):
    count, mine = (lax.axis_size(axis), lax.axis_index(axis))
    pieces = jax.tree.map(lambda part: lax.all_gather(part, axis), value)
    total = jax.tree.map(
        lambda part, zero: jnp.full_like(part, 0) + jnp.asarray(zero, part.dtype), value, neutral
    )

    def turn(position, total):
        longer = join(total, jax.tree.map(lambda part: part[position], pieces))
        return jax.tree.map(lambda new, old: jnp.where(position < mine, new, old), longer, total)

    return lax.fori_loop(0, count - 1, turn, total)


def entering(array, axis, join, neutral):
    count = lax.axis_size(axis)
    place = lax.axis_index(axis)
    ahead = count - 1 - place
    gathered = jax.tree.map(
        lambda a, kind: lax.all_gather(a.astype(kind), axis),
        array,
        jax.tree.map(lambda a: jnp.bfloat16 if a.dtype == jnp.float32 else a.dtype, array),
    )
    state = jax.tree.map(lambda a, e: jnp.zeros_like(a) + jnp.asarray(e, a.dtype), array, neutral)

    def one(turn, state):
        source = count - 1 - turn
        return join(
            state,
            jax.tree.map(
                lambda a, own: lax.dynamic_index_in_dim(a, source, 0, False).astype(own.dtype),
                gathered,
                array,
            ),
        )

    return lax.fori_loop(0, ahead, one, state)


def product_exact(left, right):
    return jnp.dot(left, right, precision=lax.Precision.HIGHEST)


def product_plain(left, right):
    return jnp.dot(left, right, preferred_element_type=jnp.float32)


def product_lead(left, right):
    return lax.dot_general(
        left, right, (((0,), (0,)), ((), ())), preferred_element_type=jnp.float32
    )


def product_last(left, right):
    return lax.dot_general(
        left, right, (((1,), (1,)), ((), ())), preferred_element_type=jnp.float32
    )


def rms_norm(values, gain):
    return values * lax.rsqrt(jnp.mean(values * values, axis=-1, keepdims=True) + norm_eps) * gain


def gate_norm(attended, gain, out_gate):
    return rms_norm(attended, gain) * jax.nn.silu(out_gate)


def swiglu(gate_up_val):
    half_width = gate_up_val.shape[1] // 2
    return jax.nn.silu(gate_up_val[:, :half_width]) * gate_up_val[:, half_width:]


def decay_of(logits):
    return jax.nn.log_sigmoid(logits) / 16.0


def span_step(carried, pieces):
    queries, key_rows, value_rows, log_decay = pieces
    cumulative = jnp.cumsum(log_decay, axis=0)
    positions = jnp.arange(queries.shape[0])
    causal = positions[:, None] >= positions[None, :]
    query_in = queries * jnp.exp(cumulative)
    scores = jnp.where(causal, product_exact(query_in, (key_rows * jnp.exp(-cumulative)).T), 0.0)
    outputs = product_exact(scores, value_rows) + product_exact(query_in, carried)
    ending = cumulative[-1]
    carried = jnp.exp(ending)[:, None] * carried + product_exact(
        (key_rows * jnp.exp(ending - cumulative)).T, value_rows
    )
    return (carried, outputs)


def core_local(queries, key_rows, value_rows, log_decay, state_in):
    blocks = queries.shape[0] // SPAN
    scaled = queries * queries.shape[1] ** (-0.5)
    pieces = (
        scaled.reshape(blocks, SPAN, -1),
        key_rows.reshape(blocks, SPAN, -1),
        value_rows.reshape(blocks, SPAN, -1),
        log_decay.reshape(blocks, SPAN, -1),
    )
    ending, outputs = lax.scan(span_step, state_in, pieces)
    return (outputs.reshape(queries.shape[0], -1), ending)


def join_states(earlier, later):
    return (earlier[0] + later[0], jnp.exp(later[0])[:, None] * earlier[1] + later[1])


def join_grads(earlier, later):
    return (earlier[0] + later[0], later[1] + jnp.exp(later[0])[:, None] * earlier[1])


def on_device(
    tokens,
    attn_gain,
    w_in,
    conv_weight,
    gate_down,
    gate_up,
    forget_bias,
    out_gain,
    w_out,
    mlp_gain,
    w_gate_up,
    w_down,
    cotangent,
):
    tok_count = tokens.shape[0]
    qkv_width = conv_weight.shape[1]
    key_width = gate_up.shape[1]
    value_width = out_gain.shape[0]
    rim_rows = conv_weight.shape[0] - 1
    inputs = tokens.astype(jnp.float32)
    attn_gain32 = attn_gain.astype(jnp.float32)
    normed32, attn_norm_back = jax.vjp(rms_norm, inputs, attn_gain32)
    normed = normed32.astype(jnp.bfloat16)
    projected = product_plain(normed, w_in)
    mixed_pre = projected[:, :qkv_width].astype(jnp.bfloat16)
    out_gate = projected[:, qkv_width:]
    prev_rows = from_behind(mixed_pre[tok_count - rim_rows :], "seq", 1)
    extended = jnp.concatenate([prev_rows, mixed_pre], axis=0).astype(jnp.float32)
    kernel = conv_weight.astype(jnp.float32)
    conv_pre = jnp.zeros((tok_count, qkv_width), jnp.float32)
    for offset in range(rim_rows + 1):
        conv_pre = conv_pre + kernel[offset] * extended[offset : offset + tok_count]
    activated, silu_back = jax.vjp(jax.nn.silu, conv_pre)
    convolved = lax.optimization_barrier(activated.astype(jnp.bfloat16)).astype(jnp.float32)
    queries = convolved[:, :key_width]
    key_rows = convolved[:, key_width : 2 * key_width]
    value_rows = convolved[:, 2 * key_width :]
    low_rank = product_plain(normed, gate_down)
    gate_up32 = gate_up.astype(jnp.float32)
    logits = product_exact(low_rank, gate_up32) + forget_bias.astype(jnp.float32)
    log_decay, decay_back = jax.vjp(decay_of, logits)
    cumulative = jnp.cumsum(log_decay, axis=0)
    block_decay = cumulative[-1]
    local_state = product_exact((key_rows * jnp.exp(block_decay - cumulative)).T, value_rows)
    empty_state = (
        jnp.zeros((key_width,), jnp.float32),
        jnp.zeros((key_width, value_width), jnp.float32),
    )
    prefix = prefix_2((block_decay, local_state), "seq", join_states, empty_state)
    (attended, final_state), core_back = jax.vjp(
        core_local, queries, key_rows, value_rows, log_decay, prefix[1]
    )
    out_gain32 = out_gain.astype(jnp.float32)
    gated32, gate_back = jax.vjp(gate_norm, attended, out_gain32, out_gate)
    gated = gated32.astype(jnp.bfloat16)
    mixer_total = lax.psum(product_plain(gated, w_out), "head")
    residual = inputs + mixer_total
    mlp_gain32 = mlp_gain.astype(jnp.float32)
    normed_mlp32, mlp_norm_back = jax.vjp(rms_norm, residual, mlp_gain32)
    normed_mlp = normed_mlp32.astype(jnp.bfloat16)
    gate_up_val = product_plain(normed_mlp, w_gate_up)
    hidden32, act_back = jax.vjp(swiglu, gate_up_val)
    hidden = hidden32.astype(jnp.bfloat16)
    mlp_total = lax.psum(product_plain(hidden, w_down).astype(jnp.bfloat16), "head").astype(
        jnp.float32
    )
    block_out = (residual + mlp_total).astype(jnp.bfloat16)
    grad_w_down = product_lead(hidden, cotangent)
    grad_hidden = product_last(cotangent, w_down)
    grad_gate_up_val = act_back(grad_hidden)[0].astype(jnp.bfloat16)
    grad_w_gate_up = product_lead(normed_mlp, grad_gate_up_val)
    normed_mlp_grad = lax.psum(
        product_last(grad_gate_up_val, w_gate_up).astype(jnp.bfloat16), "head"
    ).astype(jnp.float32)
    grad_resid_part, grad_mlp_gain = mlp_norm_back(normed_mlp_grad)
    grad_residual = cotangent.astype(jnp.float32) + grad_resid_part
    grad_res_low = grad_residual.astype(jnp.bfloat16)
    grad_w_out = product_lead(gated, grad_res_low)
    grad_gated = product_last(grad_res_low, w_out)
    grad_attended, grad_out_gain, grad_out_gate = gate_back(grad_gated)
    scaled_query = queries * key_width ** (-0.5) * jnp.exp(cumulative)
    state_from_out = product_exact(scaled_query.T, grad_attended)
    suffix = entering((block_decay, state_from_out), "seq", join_grads, empty_state)
    grad_queries, grad_keys, grad_values, grad_decay, unused_state = core_back(
        (grad_attended, suffix[1])
    )
    grad_convolved = jnp.concatenate([grad_queries, grad_keys, grad_values], axis=1)
    grad_conv_pre = silu_back(grad_convolved)[0]
    grad_extended = jnp.zeros((tok_count + rim_rows, qkv_width), jnp.float32)
    kernel_rows = []
    for offset in range(rim_rows + 1):
        grad_extended = grad_extended + jnp.pad(
            kernel[offset] * grad_conv_pre, ((offset, rim_rows - offset), (0, 0))
        )
        kernel_rows.append(jnp.sum(extended[offset : offset + tok_count] * grad_conv_pre, axis=0))
    grad_kernel = jnp.stack(kernel_rows, axis=0)
    next_rows = from_behind(grad_extended[:rim_rows], "seq", -1)
    grad_pre = grad_extended[rim_rows:] + jnp.pad(next_rows, ((tok_count - rim_rows, 0), (0, 0)))
    grad_projected = jnp.concatenate([grad_pre, grad_out_gate], axis=1).astype(jnp.bfloat16)
    grad_w_in = product_lead(normed, grad_projected)
    normed_grad_part = product_last(grad_projected, w_in)
    grad_logits = decay_back(grad_decay)[0]
    grad_forget_bias = jnp.sum(grad_logits, axis=0)
    grad_gate_up = product_exact(low_rank.T, grad_logits)
    grad_low_rank = product_exact(grad_logits, gate_up32.T)
    summed_normed, summed_low_rank, summed_out_gain = (
        lax.psum(normed_grad_part.astype(jnp.bfloat16), "head").astype(jnp.float32),
        lax.psum(grad_low_rank.astype(jnp.bfloat16), "head").astype(jnp.float32),
        lax.psum(grad_out_gain.astype(jnp.bfloat16), "head").astype(jnp.float32),
    )
    normed_wide = normed.astype(jnp.float32)
    grad_gate_down = product_exact(normed_wide.T, summed_low_rank)
    total_normed = summed_normed + product_exact(summed_low_rank, gate_down.astype(jnp.float32).T)
    grad_input_part, grad_attn_gain = attn_norm_back(total_normed)
    grad_tokens = (grad_residual + grad_input_part).astype(jnp.bfloat16)
    reduced = (
        lax.psum_scatter(grad_w_in, "seq", scatter_dimension=0, tiled=True),
        lax.psum_scatter(grad_gate_down, "seq", scatter_dimension=0, tiled=True),
        lax.psum_scatter(grad_w_out, "seq", scatter_dimension=1, tiled=True),
        lax.psum_scatter(grad_attn_gain, "seq", scatter_dimension=0, tiled=True),
        lax.psum_scatter(grad_w_gate_up, "seq", scatter_dimension=0, tiled=True),
        lax.psum_scatter(grad_w_down, "seq", scatter_dimension=1, tiled=True),
        lax.psum_scatter(grad_mlp_gain, "seq", scatter_dimension=0, tiled=True),
    )
    small_sums = lax.psum((grad_kernel, grad_gate_up, grad_forget_bias, summed_out_gain), "seq")
    return (
        block_out,
        grad_tokens,
        reduced[3],
        reduced[0],
        small_sums[0],
        reduced[1],
        small_sums[1],
        small_sums[2],
        small_sums[3],
        reduced[2],
        reduced[6],
        reduced[4],
        reduced[5],
    )


def solution(mesh):
    return jax.shard_map(
        on_device,
        mesh=mesh,
        in_specs=(
            P("seq", None),
            P(),
            P(None, "head"),
            P(None, "head"),
            P(),
            P(None, "head"),
            P("head"),
            P(),
            P("head", None),
            P(),
            P(None, "head"),
            P("head", None),
            P("seq", None),
        ),
        out_specs=(
            P("seq", None),
            P("seq", None),
            P("seq"),
            P("seq", "head"),
            P(None, "head"),
            P("seq", None),
            P(None, "head"),
            P("head"),
            P(),
            P("head", "seq"),
            P("seq"),
            P("seq", "head"),
            P("head", "seq"),
        ),
        check_vma=False,
    )
```

profile of v0, /device:TPU:0, one launch (start us, length us, event | category | flops | bytes accessed | tf_op | source)
XLA Modules:
  0.0 801.7 jit_solution(14223461639726188271)
XLA Ops:
  9.9 3.1 fusion.161
  13.1 4.8 collective-permute-start
  25.5 20.5 %all-gather.2 = f32[8,1,128]{2,1,0:T(1,128)} all-gather(f32[1,1,128]{2,1,0:T(1,128)} %get-tuple-element.1097), channel_id=1, replica_groups=mesh['seq'=8,'head'=4] {'seq'}, dimensions={0}, use_global_device_ids=true | all-gather | bytes 4608 | tf_op jit(solution)/shard_map/all_gather | solution.py:20
  46.0 1.6 negate_multiply_fusion
  49.1 1.6 slice.118
  50.8 1.6 slice_multiply_fusion
  52.3 12.5 %all-gather.6.cloned.1.call-done = f32[1024,256]{1,0:T(8,128)} async-done(((f32[128,256]{1,0:T(8,128)}), f32[1024,256]{1,0:T(8,128)}) %all-gather.6.cloned.1.call-update) | async-done | bytes 1048592 | tf_op jit(solution)/shard_map/all_gather | solution.py:20
  64.8 15.5 %while.88 = (s32[]{:T(128)}, f32[128,256]{1,0:T(8,128)S(1)}, s32[]{:T(128)}, f32[8,128]{1,0:T(8,128)}, f32[8,128,256]{2,1,0:T(8,128)}, /*index=5*/s32[]{:T(128)}, s32[]{:T(128)}) while((s32[]{:T(128)}, f32[128,256]{1,0:T(8,128)S(1)}, s32[]{:T(128)}, f32[8,128]{1,0:T(8,128)}, f32[8,128,256]{2,1,0:T(8,128)}, /*index=5*/s32[]{:T(128)}, ...), condition=%wide.region_4.5_spmd.clone, body=%wide.region_3.4_spmd.clone.sunk | while | flops 131076 | bytes 394865 | solution.py:29
  83.7 65.2 %while.86 = (s32[]{:T(128)}, f32[128,256]{1,0:T(8,128)S(1)}, f32[4,64,256]{2,1,0:T(8,128)}, f32[4,64,128]{2,1,0:T(8,128)}, f32[4,64,128]{2,1,0:T(8,128)}, /*inde...) while((s32[]{:T(128)}, f32[128,256]{1,0:T(8,128)S(1)}, ...), condition=%wide.region_7.8_spmd.clone, body=%wide.region_5.7_spmd.clone.sunk | while | flops 69918720 | bytes 1779933 | solution.py:118
  87.2 1.6 bitcast_dynamic-update-slice_fusion.11
  89.8 1.6 fusion.231
  103.5 1.6 bitcast_dynamic-update-slice_fusion.11
  106.2 1.6 fusion.231
  119.8 1.6 bitcast_dynamic-update-slice_fusion.11
  122.5 1.6 fusion.231
  136.1 1.6 bitcast_dynamic-update-slice_fusion.11
  138.8 1.6 fusion.231
  153.1 2.3 fusion.162
  156.8 18.2 %all-gather.3 = bf16[8,1,128]{2,1,0:T(2,128)(2,1)S(1)} all-gather(bf16[1,1,128]{2,1,0:T(2,128)(2,1)S(1)} %convert_bitcast_fusion), channel_id=1, replica_groups=mesh['seq'=8,'head'=4] {'seq'}, dimensions={0}, use_global_device_ids=true | all-gather | bytes 2304 | tf_op jit(solution)/shard_map/all_gather | solution.py:37
  175.6 14.8 %all-reduce.17.cloned.1.call-done = f32[256,1024]{1,0:T(8,128)} async-done(((f32[256,1024]{1,0:T(8,128)}), f32[256,1024]{1,0:T(8,128)}) %all-reduce.17.cloned.1.call-update) | async-done | bytes 1048592 | tf_op jit(solution)/shard_map/psum | solution.py:186
  190.4 1.6 multiply_reduce_fusion
  194.7 1.6 fusion.138
  197.4 1.8 convolution_convert_fusion
  199.3 2.9 convolution_convert_fusion.2
  202.2 30.8 %all-reduce.19.cloned.1.call-done = bf16[256,1024]{1,0:T(8,128)(2,1)} async-done(((bf16[256,1024]{1,0:T(8,128)(2,1)}), bf16[256,1024]{1,0:T(8,128)(2,1)}) %all-reduce.19.cloned.1.call-update) | async-done | bytes 524304 | tf_op jit(solution)/shard_map/psum | solution.py:202
  233.0 2.4 fusion.94
  240.3 33.4 %all-gather.1 = bf16[1024,256]{1,0:T(8,128)(2,1)} all-gather(bf16[128,256]{1,0:T(8,128)(2,1)S(1)} %convolution_convert_fusion.3), channel_id=3, replica_groups=mesh['seq'=8,'head'=4] {'seq'}, dimensions={0}, use_global_device_ids=true | all-gather | bytes 589824 | tf_op jit(solution)/shard_map/all_gather | solution.py:37
  273.7 11.6 %while.85 = (s32[]{:T(128)}, f32[128,256]{1,0:T(8,128)S(1)}, s32[]{:T(128)}, bf16[8,128,256]{2,1,0:T(8,128)(2,1)}, bf16[8,128]{1,0:T(8,128)(2,1)}, /*index=5*/s32[]{:T(128)}, s32[]{:T(128)}, s32[]{:T(128)}, s32[]{:T(128)}) while((s32[]{:T(128)}, f32[128,256]{1,0:T(8,128)S(1)}, s32[]{:T(128)}, bf16[8,128,256]{2,1,0:T(8,128)(2,1)}, ...), condition=%wide.region_16.17_spmd, body=%wide.region_15.16_spmd.sunk | while | flops 98438 | bytes 329115 | solution.py:54
  288.0 69.5 %while.87 = (s32[]{:T(128)}, f32[128,256]{1,0:T(8,128)S(1)}, f32[4,64,128]{2,1,0:T(8,128)}, f32[4,64,128]{2,1,0:T(8,128)}, f32[4,64,256]{2,1,0:T(8,128)}, /*inde...) while((s32[]{:T(128)}, f32[128,256]{1,0:T(8,128)S(1)}, ...), condition=%wide.region_21.22_spmd.clone, body=%wide.region_17.21_spmd.clone.sunk | while | flops 139239424 | bytes 4158289 | solution.py:118
  295.4 1.5 bitcast_dynamic-update-slice_fusion.14
  296.9 1.6 bitcast_dynamic-update-slice_fusion.15
  298.5 1.7 fusion.250
  302.4 1.6 reduce_window_sum.53
  312.8 1.5 bitcast_dynamic-update-slice_fusion.14
  314.3 1.6 bitcast_dynamic-update-slice_fusion.15
  315.9 1.7 fusion.250
  319.8 1.6 reduce_window_sum.53
  330.2 1.5 bitcast_dynamic-update-slice_fusion.14
  331.7 1.6 bitcast_dynamic-update-slice_fusion.15
  333.3 1.7 fusion.250
  337.2 1.6 reduce_window_sum.53
  347.5 1.5 bitcast_dynamic-update-slice_fusion.14
  349.1 1.6 bitcast_dynamic-update-slice_fusion.15
  350.7 1.7 fusion.250
  354.5 1.6 reduce_window_sum.53
  357.5 1.6 multiply_negate_fusion
  359.2 2.2 multiply_reduce_fusion.4
  361.7 1.6 collective-permute-start.1
  363.6 3.8 collective-permute-done.1
  369.7 1.6 fusion.157
  372.1 7.5 all-reduce.11
  379.6 1.6 fusion.150
  381.3 2.6 fusion.110
  384.0 3.3 fusion.163
  387.4 3.4 fusion.115
  391.5 5.3 fusion.140
  402.6 2.6 fusion.92
  405.2 37.7 %all-reduce.10 = (f32[1024]{0:T(1024)S(1)}, f32[4,512]{1,0:T(4,128)}, f32[16,128]{1,0:T(8,128)}, f32[128]{0:T(128)}, f32[256]{0:T(256)}, /*index=5*/f32[1024]{0:T(1024)S(1)}) all-reduce(f32[1024]{0:T(1024)S(1)} %get-tuple-element.952, f32[4,512]{1,0:T(4,128)S(1)} %copy-done.36, ...), channel_id=4, replica_groups=mesh['seq'=8,'head'=4] {'seq'}, use_global_device_ids=true, to_apply=%region_26.27.clone | all-reduce | flops 6528 | bytes 51712
  444.7 2.3 add_convert_fusion.1
  448.2 12.1 %reduce-scatter.8.cloned.1.call-done = f32[128,16]{0,1:T(8,128)} async-done(((f32[1024,16]{0,1:T(8,128)}), f32[128,16]{0,1:T(8,128)}) %reduce-scatter.8.cloned.1.call-update) | async-done | bytes 8208 | tf_op jit(solution)/shard_map/reduce_scatter | solution.py:248
  460.3 66.9 %reduce-scatter.10.cloned.1.call-done = f32[256,128]{1,0:T(8,128)} async-done(((f32[256,1024]{1,0:T(8,128)}), f32[256,128]{1,0:T(8,128)}) %reduce-scatter.10.cloned.1.call-update) | async-done | bytes 131088 | tf_op jit(solution)/shard_map/reduce_scatter | solution.py:249
  527.2 75.9 %reduce-scatter.14.cloned.1.call-done = f32[704,128]{1,0:T(8,128)} async-done(((f32[704,1024]{1,0:T(8,128)}), f32[704,128]{1,0:T(8,128)}) %reduce-scatter.14.cloned.1.call-update) | async-done | bytes 360464 | tf_op jit(solution)/shard_map/reduce_scatter | solution.py:252
  603.1 78.2 %reduce-scatter.6.cloned.1.call-done = f32[128,768]{1,0:T(8,128)} async-done(((f32[1024,768]{1,0:T(8,128)}), f32[128,768]{1,0:T(8,128)}) %reduce-scatter.6.cloned.1.call-update) | async-done | bytes 393232 | tf_op jit(solution)/shard_map/reduce_scatter | solution.py:247
  681.3 113.8 %reduce-scatter.12.cloned.1.call-done = f32[128,1408]{1,0:T(8,128)} async-done(((f32[1024,1408]{1,0:T(8,128)}), f32[128,1408]{1,0:T(8,128)}) %reduce-scatter.12.cloned.1.call-update) | async-done | bytes 720912 | tf_op jit(solution)/shard_map/reduce_scatter | solution.py:251
  (352 shorter events, 167.0 us)
Async XLA Ops:
  7.2 186.0 %copy-start = (bf16[1024,1408]{1,0:T(8,128)(2,1)S(1)}, bf16[1024,1408]{1,0:T(8,128)(2,1)}, u32[]{:S(2)}) copy-start(bf16[1024,1408]{1,0:T(8,128)(2,1)} %param.31) | copy-start | bytes 8650756
  7.2 57.6 %all-gather.6.cloned.1.call-start = ((), (), s32[]{:S(2)}) async-start(), calls=%async_computation.12 | async-start | bytes 1179648 | tf_op jit(solution)/shard_map/all_gather | solution.py:20
  8.1 9.9 %copy-start.34 = (f32[1024]{0:T(1024)}, f32[1024]{0:T(1024)S(1)}, u32[]{:S(2)}) copy-start(f32[1024]{0:T(1024)S(1)} %convert_element_type.127) | copy-start | bytes 12292
  9.9 8.1 %copy-start.48 = (f32[256]{0:T(256)}, f32[256]{0:T(256)S(1)}, u32[]{:S(2)}) copy-start(f32[256]{0:T(256)S(1)} %fusion.142) | copy-start | bytes 3076
  9.9 8.0 %copy-start.65 = (bf16[128]{0:T(256)(128)(2,1)S(1)}, bf16[128]{0:T(256)(128)(2,1)}, u32[]{:S(2)}) copy-start(bf16[128]{0:T(256)(128)(2,1)} %param.27) | copy-start | bytes 772
  9.9 8.1 %copy-start.3 = (bf16[256,1024]{1,0:T(8,128)(2,1)S(1)}, bf16[256,1024]{1,0:T(8,128)(2,1)}, u32[]{:S(2)}) copy-start(bf16[256,1024]{1,0:T(8,128)(2,1)} %param.21) | copy-start | bytes 1572868
  9.9 8.1 %copy-start.64 = (bf16[1024,16]{0,1:T(8,128)(2,1)S(1)}, bf16[1024,16]{0,1:T(8,128)(2,1)}, u32[]{:S(2)}) copy-start(bf16[1024,16]{0,1:T(8,128)(2,1)} %param.25) | copy-start | bytes 98308
  9.9 8.4 %copy-start.60 = (bf16[16,128]{1,0:T(8,128)(2,1)S(1)}, bf16[16,128]{1,0:T(8,128)(2,1)}, u32[]{:S(2)}) copy-start(bf16[16,128]{1,0:T(8,128)(2,1)} %param.26) | copy-start | bytes 12292
  13.1 5.2 copy-start.21
  13.1 6.5 copy-start.47
  13.1 8.0 %collective-permute-start = (bf16[3,512]{1,0:T(4,128)(2,1)S(1)}, bf16[3,512]{1,0:T(4,128)(2,1)S(1)}, u32[]{:S(2)}, u32[]{:S(2)}) collective-permute-start(bf16[3,512]{1,0:T(4,128)(2,1)S(1)} %slice.107), channel_id=1, source_target_pairs={{0,4},{4,8},{8,12},{12,16},{16,20},{20,24},{24,28},{1,5},{5,9},{9,... | collective-permute-start | bytes 9224 | tf_op jit(solution)/shard_map/ppermute | solution.py:15
  19.5 2.8 copy-start.18
  19.6 2.7 copy-start.37
  19.6 2.7 copy-start.39
  19.6 2.7 copy-start.41
  19.6 2.7 copy-start.43
  24.2 166.3 %all-reduce.17.cloned.1.call-start = ((), (), s32[]{:S(2)}) async-start(), calls=%async_computation.5 | async-start | bytes 2097152 | tf_op jit(solution)/shard_map/psum | solution.py:186
  151.3 5.5 copy-start.19
  155.4 77.6 %all-reduce.19.cloned.1.call-start = ((), (), s32[]{:S(2)}) async-start(), calls=%async_computation.6 | async-start | bytes 1048576 | tf_op jit(solution)/shard_map/psum | solution.py:202
  190.4 2.8 copy-start.28
  199.3 203.3 %all-reduce.21.cloned.1.call-start = ((), (), s32[]{:S(2)}) async-start(), calls=%async_computation.13 | async-start | bytes 2097152 | tf_op jit(solution)/shard_map/psum | solution.py:194
  233.0 2.4 copy-start.53
  233.0 2.4 copy-start.2
  233.0 2.4 copy-start.12
  233.0 2.4 copy-start.29
  233.0 2.5 copy-start.32
  235.5 1.5 copy-start.8
  237.1 1.8 copy-start.6
  238.9 34.8 %copy-start.5 = (f32[256,256]{1,0:T(8,128)}, f32[256,256]{1,0:T(8,128)S(1)}, u32[]{:S(2)}) copy-start(f32[256,256]{1,0:T(8,128)S(1)} %get-tuple-element.1090) | copy-start | bytes 786436
  288.0 7.3 copy-start.16
  288.1 8.9 %copy-start.10 = (f32[4,64,128]{2,1,0:T(8,128)S(1)}, f32[4,64,128]{2,1,0:T(8,128)}, u32[]{:S(2)}) copy-start(f32[4,64,128]{2,1,0:T(8,128)} %get-tuple-element.1596) | copy-start | bytes 393220 | tf_op jit(solution)/shard_map/transpose(jvp())/while
  288.1 8.9 %copy-start.15 = (f32[4,64,128]{2,1,0:T(8,128)S(1)}, f32[4,64,128]{2,1,0:T(8,128)}, u32[]{:S(2)}) copy-start(f32[4,64,128]{2,1,0:T(8,128)} %get-tuple-element.1597) | copy-start | bytes 393220 | tf_op jit(solution)/shard_map/transpose(jvp())/while
  305.4 7.4 copy-start.16
  305.4 9.0 %copy-start.10 = (f32[4,64,128]{2,1,0:T(8,128)S(1)}, f32[4,64,128]{2,1,0:T(8,128)}, u32[]{:S(2)}) copy-start(f32[4,64,128]{2,1,0:T(8,128)} %get-tuple-element.1596) | copy-start | bytes 393220 | tf_op jit(solution)/shard_map/transpose(jvp())/while
  305.4 9.0 %copy-start.15 = (f32[4,64,128]{2,1,0:T(8,128)S(1)}, f32[4,64,128]{2,1,0:T(8,128)}, u32[]{:S(2)}) copy-start(f32[4,64,128]{2,1,0:T(8,128)} %get-tuple-element.1597) | copy-start | bytes 393220 | tf_op jit(solution)/shard_map/transpose(jvp())/while
  322.8 7.4 copy-start.16
  322.8 9.0 %copy-start.10 = (f32[4,64,128]{2,1,0:T(8,128)S(1)}, f32[4,64,128]{2,1,0:T(8,128)}, u32[]{:S(2)}) copy-start(f32[4,64,128]{2,1,0:T(8,128)} %get-tuple-element.1596) | copy-start | bytes 393220 | tf_op jit(solution)/shard_map/transpose(jvp())/while
  322.8 9.0 %copy-start.15 = (f32[4,64,128]{2,1,0:T(8,128)S(1)}, f32[4,64,128]{2,1,0:T(8,128)}, u32[]{:S(2)}) copy-start(f32[4,64,128]{2,1,0:T(8,128)} %get-tuple-element.1597) | copy-start | bytes 393220 | tf_op jit(solution)/shard_map/transpose(jvp())/while
  340.2 7.4 copy-start.16
  340.2 8.9 %copy-start.10 = (f32[4,64,128]{2,1,0:T(8,128)S(1)}, f32[4,64,128]{2,1,0:T(8,128)}, u32[]{:S(2)}) copy-start(f32[4,64,128]{2,1,0:T(8,128)} %get-tuple-element.1596) | copy-start | bytes 393220 | tf_op jit(solution)/shard_map/transpose(jvp())/while
  340.2 8.9 %copy-start.15 = (f32[4,64,128]{2,1,0:T(8,128)S(1)}, f32[4,64,128]{2,1,0:T(8,128)}, u32[]{:S(2)}) copy-start(f32[4,64,128]{2,1,0:T(8,128)} %get-tuple-element.1597) | copy-start | bytes 393220 | tf_op jit(solution)/shard_map/transpose(jvp())/while
  359.2 2.2 copy-start.38
  359.2 2.2 copy-start.40
  359.2 2.2 copy-start.42
  359.2 2.2 copy-start.44
  361.7 6.5 copy-start.17
  361.7 6.5 copy-start.27
  361.7 5.7 collective-permute-start.1
  368.2 11.5 %copy-start.4 = (bf16[256,1024]{1,0:T(8,128)(2,1)S(1)}, bf16[256,1024]{1,0:T(8,128)(2,1)}, u32[]{:S(2)}) copy-start(bf16[256,1024]{1,0:T(8,128)(2,1)} %param.21) | copy-start | bytes 1572868
  368.2 11.5 %copy-start.35 = (f32[1024]{0:T(1024)S(1)}, f32[1024]{0:T(1024)}, u32[]{:S(2)}) copy-start(f32[1024]{0:T(1024)} %copy-done.34) | copy-start | bytes 12292
  368.2 11.5 %copy-start.49 = (f32[256]{0:T(256)S(1)}, f32[256]{0:T(256)}, u32[]{:S(2)}) copy-start(f32[256]{0:T(256)} %copy-done.48) | copy-start | bytes 3076
  369.6 90.7 %reduce-scatter.8.cloned.1.call-start = ((), (), s32[]{:S(2)}) async-start(), calls=%async_computation.8 | async-start | bytes 73728 | tf_op jit(solution)/shard_map/reduce_scatter | solution.py:248
  381.3 145.9 %reduce-scatter.10.cloned.1.call-start = ((), (), s32[]{:S(2)}) async-start(), calls=%async_computation.9 | async-start | bytes 1179648 | tf_op jit(solution)/shard_map/reduce_scatter | solution.py:249
  384.0 219.1 %reduce-scatter.14.cloned.1.call-start = ((), (), s32[]{:S(2)}) async-start(), calls=%async_computation.11 | async-start | bytes 3244032 | tf_op jit(solution)/shard_map/reduce_scatter | solution.py:252
  387.3 294.0 %reduce-scatter.6.cloned.1.call-start = ((), (), s32[]{:S(2)}) async-start(), calls=%async_computation.7 | async-start | bytes 3538944 | tf_op jit(solution)/shard_map/reduce_scatter | solution.py:247
  390.8 404.3 %reduce-scatter.12.cloned.1.call-start = ((), (), s32[]{:S(2)}) async-start(), calls=%async_computation.10 | async-start | bytes 6488064 | tf_op jit(solution)/shard_map/reduce_scatter | solution.py:251
  396.8 3.1 copy-start.58
  396.9 3.1 copy-start.59
  396.9 8.3 %copy-start.45 = (f32[1024]{0:T(1024)S(1)}, f32[1024]{0:T(1024)}, u32[]{:S(2)}) copy-start(f32[1024]{0:T(1024)} %get-tuple-element.950) | copy-start | bytes 12292
  402.2 3.0 copy-start.36
  402.2 3.0 copy-start.62
  405.2 41.9 %copy-start.50 = (f32[256]{0:T(256)S(1)}, f32[256]{0:T(256)}, u32[]{:S(2)}) copy-start(f32[256]{0:T(256)} %copy-done.48) | copy-start | bytes 3076
  442.9 4.2 copy-start.7
  442.9 4.2 copy-start.22
  (22 other events, 21.0 us)
Sparse Core Ops, SparseCore 0:
  24.3 40.4 all-gather.5
  155.6 34.8 all-reduce.16
  199.4 33.5 all-reduce.18
  369.7 32.8 all-reduce.20
  406.2 54.0 reduce-scatter.7
  464.1 63.0 reduce-scatter.9
  531.7 71.3 reduce-scatter.13
  607.7 73.6 reduce-scatter.5
  686.0 109.0 reduce-scatter.11
where the time goes:
time: 809 us; the launch traced here: 802 us
  waiting for transfers between devices  409 us (51%)
  blocking collectives  117 us (14%)
  matrix products  103 us (13%)
  other arithmetic  85.1 us (11%)
  local copies, waits for them, and re-layouts  63.7 us (8%)
  between operations  15.2 us (2%)
    reduce_scatter x1, waiting for transfers between devices, on_device(): lax.psum_scatter(grad_w_gate_up, 'seq', scatter_dimension=0, tiled=True)  114 us
    reduce_scatter x1, waiting for transfers between devices, on_device(): lax.psum_scatter(grad_w_in, 'seq', scatter_dimension=0, tiled=True)  78.2 us
    reduce_scatter x1, waiting for transfers between devices, on_device(): lax.psum_scatter(grad_w_down, 'seq', scatter_dimension=1, tiled=True)  75.9 us
    dot_general x55, matrix products, product_exact(): return jnp.dot(left, right, precision=lax.Precision.HIGHEST)  73.4 us
    reduce_scatter x1, waiting for transfers between devices, on_device(): lax.psum_scatter(grad_w_out, 'seq', scatter_dimension=1, tiled=True)  66.9 us
    all_gather x2, blocking collectives, entering(): lax.all_gather(a.astype(kind), axis)  51.6 us
    unnamed x1, blocking collectives  37.7 us
    psum x1, waiting for transfers between devices, on_device(): lax.psum(product_last(grad_gate_up_val, w_gate_up).astype(jnp.bfloat16),...  30.8 us
  transfers between devices with their start and end apart: 11, of which 10 were waited for; matrix products, arithmetic and copies ran while one was open for 6% of the time, Pallas kernels for 0%

commit v1 on v0

v1 whole, which is shorter than its diff:
```python
import functools

import jax
import jax.numpy as jnp
from jax import lax
from jax.experimental import pallas as pl
from jax.experimental.pallas import tpu as pltpu
from jax.sharding import PartitionSpec as P

SPAN = 64


norm_eps = 1e-05

MESH = pl.DeviceIdType.MESH
LIMIT = 24 * 1024 * 1024
low_type = jnp.bfloat16


def from_behind(value, axis, steps):
    count = lax.axis_size(axis)
    leading, last = (max(0, -steps), min(count, count - steps))
    return lax.ppermute(value, axis, [(source, source + steps) for source in range(leading, last)])


def product_exact(left, right):
    return jnp.dot(left, right, precision=lax.Precision.HIGHEST)


def product_plain(left, right):
    return jnp.dot(left, right, preferred_element_type=jnp.float32)


def product_lead(left, right):
    return lax.dot_general(
        left, right, (((0,), (0,)), ((), ())), preferred_element_type=jnp.float32
    )


def product_last(left, right):
    return lax.dot_general(
        left, right, (((1,), (1,)), ((), ())), preferred_element_type=jnp.float32
    )


def rms_norm(values, gain):
    return values * lax.rsqrt(jnp.mean(values * values, axis=-1, keepdims=True) + norm_eps) * gain


def gate_norm(attended, gain, out_gate):
    return rms_norm(attended, gain) * jax.nn.silu(out_gate)


def swiglu(gate_up_val):
    half_width = gate_up_val.shape[1] // 2
    return jax.nn.silu(gate_up_val[:, :half_width]) * gate_up_val[:, half_width:]


def decay_of(logits):
    return jax.nn.log_sigmoid(logits) / 16.0


def greet(axis, peers):
    barrier = pltpu.get_barrier_semaphore()
    for peer in peers:
        pl.semaphore_signal(barrier, inc=1, device_id={axis: peer}, device_id_type=MESH)
    pl.semaphore_wait(barrier, len(peers))


def comm_params(collective):
    return pltpu.CompilerParams(
        collective_id=collective, has_side_effects=True, vmem_limit_bytes=LIMIT
    )


def vmem_specs(count):
    return [pl.BlockSpec(memory_space=pltpu.VMEM)] * count


def head_sum_kernel(pieces, x_ref, o_ref, s1, r1, s2, r2, s3, r3, send, recv):
    me = lax.axis_index("head")
    near = me + 1 - 2 * lax.rem(me, 2)
    far = lax.rem(me + 2, 4)
    half = x_ref.shape[0] // 2
    step = half // pieces
    mine = lax.rem(me, 2) * half
    other = half - mine
    greet("head", (near, far))

    def copy(stage, piece, source, target, peer):
        return pltpu.make_async_remote_copy(
            src_ref=source.at[pl.ds(piece * step, step)],
            dst_ref=target.at[pl.ds(piece * step, step)],
            send_sem=send.at[stage, piece],
            recv_sem=recv.at[stage, piece],
            device_id={"head": peer},
            device_id_type=MESH,
        )

    def rows(base, piece):
        return pl.ds(pl.multiple_of(base + piece * step, 16), step)

    copies = []
    for piece in range(pieces):
        local = pl.ds(piece * step, step)
        s1[local, :] = x_ref[rows(other, piece), :].astype(low_type)
        copies.append(copy(0, piece, s1, r1, near))
        copies[-1].start()
    second = []
    for piece in range(pieces):
        local = pl.ds(piece * step, step)
        copies[piece].wait()
        s2[local, :] = (x_ref[rows(mine, piece), :] + r1[local, :].astype(jnp.float32)).astype(
            low_type
        )
        second.append(copy(1, piece, s2, r2, far))
        second[-1].start()
    third = []
    for piece in range(pieces):
        local = pl.ds(piece * step, step)
        second[piece].wait()
        total = s2[local, :].astype(jnp.float32) + r2[local, :].astype(jnp.float32)
        s3[local, :] = total
        third.append(copy(2, piece, s3, r3, near))
        third[-1].start()
        o_ref[rows(mine, piece), :] = total
    for piece in range(pieces):
        local = pl.ds(piece * step, step)
        third[piece].wait()
        o_ref[rows(other, piece), :] = r3[local, :]


def head_sum(value, collective, pieces=4):
    rows, width = value.shape
    half = (rows // 2, width)
    return pl.pallas_call(
        functools.partial(head_sum_kernel, pieces),
        out_shape=jax.ShapeDtypeStruct(value.shape, jnp.float32),
        in_specs=vmem_specs(1),
        out_specs=vmem_specs(1)[0],
        scratch_shapes=[
            pltpu.VMEM(half, low_type),
            pltpu.VMEM(half, low_type),
            pltpu.VMEM(half, low_type),
            pltpu.VMEM(half, low_type),
            pltpu.VMEM(half, jnp.float32),
            pltpu.VMEM(half, jnp.float32),
            pltpu.SemaphoreType.DMA((3, pieces)),
            pltpu.SemaphoreType.DMA((3, pieces)),
        ],
        compiler_params=comm_params(collective),
        cost_estimate=pl.CostEstimate(flops=0, bytes_accessed=40_000_000, transcendentals=0),
    )(value)


def seq_peers(count):
    me = lax.axis_index("seq")
    return [lax.rem(me + distance, count) for distance in range(1, count)]


def seq_copies(count, source_of, gathered, send, recv):
    me = lax.axis_index("seq")
    return [
        pltpu.make_async_remote_copy(
            src_ref=source_of(peer),
            dst_ref=gathered.at[me],
            send_sem=send.at[place],
            recv_sem=recv.at[place],
            device_id={"seq": peer},
            device_id_type=MESH,
        )
        for place, peer in enumerate(seq_peers(count))
    ]


def seq_sum_kernel(count, x_ref, o_ref, gathered, send, recv):
    me = lax.axis_index("seq")
    greet("seq", seq_peers(count))
    copies = seq_copies(count, lambda peer: x_ref.at[peer], gathered, send, recv)
    for one in copies:
        one.start()
    gathered[me] = x_ref[me]
    for one in copies:
        one.wait()
    total = gathered[0]
    for place in range(1, count):
        total = total + gathered[place]
    o_ref[...] = total


def seq_sum(value, collective):
    count, rows, width = value.shape
    return pl.pallas_call(
        functools.partial(seq_sum_kernel, count),
        out_shape=jax.ShapeDtypeStruct((rows, width), jnp.float32),
        in_specs=vmem_specs(1),
        out_specs=vmem_specs(1)[0],
        scratch_shapes=[
            pltpu.VMEM((count, rows, width), jnp.float32),
            pltpu.SemaphoreType.DMA((count - 1,)),
            pltpu.SemaphoreType.DMA((count - 1,)),
        ],
        compiler_params=comm_params(collective),
        cost_estimate=pl.CostEstimate(flops=0, bytes_accessed=20_000_000, transcendentals=0),
    )(value)


def dot_exact(left, right, left_dim, right_dim):
    return lax.dot_general(
        left,
        right,
        (((left_dim,), (right_dim,)), ((), ())),
        precision=lax.Precision.HIGHEST,
        preferred_element_type=jnp.float32,
    )


def causal_mask(size):
    row = lax.broadcasted_iota(jnp.int32, (size, size), 0)
    column = lax.broadcasted_iota(jnp.int32, (size, size), 1)
    return row >= column


def put_state(gathered, me, state, decay):
    height, width = state.shape
    high = decay.astype(low_type).astype(jnp.float32)
    rest = decay - high
    middle = rest.astype(low_type).astype(jnp.float32)
    last = rest - middle
    place = lax.broadcasted_iota(jnp.int32, (16, width), 0)
    extra = jnp.where(place == 0, high, jnp.where(place == 1, middle, jnp.where(place == 2, last, 0.0)))
    gathered[me, 0:height, :] = state.astype(low_type)
    gathered[me, height : height + 16, :] = extra.astype(low_type)


def join_state(total, gathered, place, taken):
    height = total.shape[0]
    extra = gathered[place, height : height + 16, :].astype(jnp.float32)
    decay = extra[0:1] + extra[1:2] + extra[2:3]
    longer = jnp.exp(decay) * total + gathered[place, 0:height, :].astype(jnp.float32)
    return jnp.where(taken, longer, total)


def mixer_forward_kernel(
    count, conv_ref, decay_ref, attended_ref, total_ref, state_ref, intra, query_in, gathered, send, recv
):
    me = lax.axis_index("seq")
    tok_count, key_width = decay_ref.shape
    spans = tok_count // SPAN
    value_width = attended_ref.shape[1]
    greet("seq", seq_peers(count))
    causal = causal_mask(SPAN)
    ones = causal.astype(jnp.float32)
    state = jnp.zeros((value_width, key_width), jnp.float32)
    before = jnp.zeros((1, key_width), jnp.float32)
    starts = []
    for span in range(spans):
        rows = pl.ds(span * SPAN, SPAN)
        cumulative = dot_exact(ones, decay_ref[rows, :], 1, 0)
        total_ref[rows, :] = cumulative
        keys = conv_ref[rows, key_width : 2 * key_width].astype(jnp.float32)
        values = conv_ref[rows, 2 * key_width :].astype(jnp.float32)
        ending = cumulative[SPAN - 1 : SPAN]
        state_ref[span] = state
        starts.append(before)
        state = jnp.exp(ending) * state + dot_exact(
            values, keys * jnp.exp(ending - cumulative), 0, 0
        )
        before = before + ending
    put_state(gathered, me, state, before)
    copies = seq_copies(count, lambda peer: gathered.at[me], gathered, send, recv)
    for one in copies:
        one.start()
    for span in range(spans):
        rows = pl.ds(span * SPAN, SPAN)
        cumulative = total_ref[rows, :]
        queries = conv_ref[rows, 0:key_width].astype(jnp.float32) * key_width ** (-0.5)
        keys = conv_ref[rows, key_width : 2 * key_width].astype(jnp.float32)
        values = conv_ref[rows, 2 * key_width :].astype(jnp.float32)
        inner = queries * jnp.exp(cumulative)
        query_in[rows, :] = inner
        scores = jnp.where(causal, dot_exact(inner, keys * jnp.exp(-cumulative), 1, 1), 0.0)
        intra[rows, :] = dot_exact(scores, values, 1, 0)
    for one in copies:
        one.wait()
    entering = jnp.zeros((value_width, key_width), jnp.float32)
    for place in range(count - 1):
        entering = join_state(entering, gathered, place, place < me)
    for span in range(spans):
        rows = pl.ds(span * SPAN, SPAN)
        start = state_ref[span] + jnp.exp(starts[span]) * entering
        state_ref[span] = start
        attended_ref[rows, :] = intra[rows, :] + dot_exact(query_in[rows, :], start, 1, 1)


def mixer_forward(convolved, log_decay, value_width, collective):
    count = lax.axis_size("seq")
    tok_count, key_width = log_decay.shape
    spans = tok_count // SPAN
    return pl.pallas_call(
        functools.partial(mixer_forward_kernel, count),
        out_shape=(
            jax.ShapeDtypeStruct((tok_count, value_width), jnp.float32),
            jax.ShapeDtypeStruct((tok_count, key_width), jnp.float32),
            jax.ShapeDtypeStruct((spans, value_width, key_width), jnp.float32),
        ),
        in_specs=vmem_specs(2),
        out_specs=tuple(vmem_specs(3)),
        scratch_shapes=[
            pltpu.VMEM((tok_count, value_width), jnp.float32),
            pltpu.VMEM((tok_count, key_width), jnp.float32),
            pltpu.VMEM((count, value_width + 16, key_width), low_type),
            pltpu.SemaphoreType.DMA((count - 1,)),
            pltpu.SemaphoreType.DMA((count - 1,)),
        ],
        compiler_params=comm_params(collective),
        cost_estimate=pl.CostEstimate(flops=0, bytes_accessed=60_000_000, transcendentals=0),
    )(convolved, log_decay)


def mixer_backward_kernel(
    count,
    conv_ref,
    total_ref,
    state_ref,
    grad_ref,
    conv_grad_ref,
    decay_grad_ref,
    local,
    gathered,
    send,
    recv,
):
    me = lax.axis_index("seq")
    tok_count, key_width = total_ref.shape
    spans = tok_count // SPAN
    value_width = grad_ref.shape[1]
    scale = key_width ** (-0.5)
    greet("seq", seq_peers(count))
    causal = causal_mask(SPAN)
    ones = causal.astype(jnp.float32)
    state = jnp.zeros((value_width, key_width), jnp.float32)
    after = jnp.zeros((1, key_width), jnp.float32)
    ends = [None] * spans
    for span in reversed(range(spans)):
        rows = pl.ds(span * SPAN, SPAN)
        cumulative = total_ref[rows, :]
        ending = cumulative[SPAN - 1 : SPAN]
        inner = conv_ref[rows, 0:key_width].astype(jnp.float32) * scale * jnp.exp(cumulative)
        local[span] = state
        ends[span] = after
        state = jnp.exp(ending) * state + dot_exact(grad_ref[rows, :], inner, 0, 0)
        after = after + ending
    put_state(gathered, me, state, after)
    copies = seq_copies(count, lambda peer: gathered.at[me], gathered, send, recv)
    for one in copies:
        one.start()
    for span in range(spans):
        rows = pl.ds(span * SPAN, SPAN)
        cumulative = total_ref[rows, :]
        inner = conv_ref[rows, 0:key_width].astype(jnp.float32) * scale * jnp.exp(cumulative)
        key_in = conv_ref[rows, key_width : 2 * key_width].astype(jnp.float32) * jnp.exp(
            -cumulative
        )
        values = conv_ref[rows, 2 * key_width :].astype(jnp.float32)
        grad = grad_ref[rows, :]
        scores = jnp.where(causal, dot_exact(inner, key_in, 1, 1), 0.0)
        grad_scores = jnp.where(causal, dot_exact(grad, values, 1, 1), 0.0)
        grad_inner = dot_exact(grad_scores, key_in, 1, 0) + dot_exact(grad, state_ref[span], 1, 0)
        grad_key_in = dot_exact(grad_scores, inner, 0, 0)
        conv_grad_ref[rows, 0:key_width] = grad_inner * (scale * jnp.exp(cumulative))
        conv_grad_ref[rows, key_width : 2 * key_width] = grad_key_in * jnp.exp(-cumulative)
        conv_grad_ref[rows, 2 * key_width :] = dot_exact(scores, grad, 0, 0)
        decay_grad_ref[rows, :] = grad_inner * inner - grad_key_in * key_in
    for one in copies:
        one.wait()
    leaving = jnp.zeros((value_width, key_width), jnp.float32)
    for turn in range(count - 1):
        place = count - 1 - turn
        leaving = join_state(leaving, gathered, place, place > me)
    for span in range(spans):
        rows = pl.ds(span * SPAN, SPAN)
        cumulative = total_ref[rows, :]
        ending = cumulative[SPAN - 1 : SPAN]
        to_end = jnp.exp(ending - cumulative)
        key_end = conv_ref[rows, key_width : 2 * key_width].astype(jnp.float32) * to_end
        values = conv_ref[rows, 2 * key_width :].astype(jnp.float32)
        out_grad = local[span] + jnp.exp(ends[span]) * leaving
        grad_key_end = dot_exact(values, out_grad, 1, 0)
        conv_grad_ref[rows, key_width : 2 * key_width] += grad_key_end * to_end
        conv_grad_ref[rows, 2 * key_width :] += dot_exact(key_end, out_grad, 1, 1)
        through = grad_key_end * key_end
        end_grad = jnp.sum(through, axis=0, keepdims=True) + jnp.exp(ending) * jnp.sum(
            state_ref[span] * out_grad, axis=0, keepdims=True
        )
        decay_grad_ref[rows, :] = (
            dot_exact(ones, decay_grad_ref[rows, :] - through, 0, 0) + end_grad
        )


def mixer_backward(convolved, cumulative, states, grad_attended, collective):
    count = lax.axis_size("seq")
    tok_count, key_width = cumulative.shape
    spans, value_width = states.shape[:2]
    return pl.pallas_call(
        functools.partial(mixer_backward_kernel, count),
        out_shape=(
            jax.ShapeDtypeStruct(convolved.shape, jnp.float32),
            jax.ShapeDtypeStruct((tok_count, key_width), jnp.float32),
        ),
        in_specs=vmem_specs(4),
        out_specs=tuple(vmem_specs(2)),
        scratch_shapes=[
            pltpu.VMEM((spans, value_width, key_width), jnp.float32),
            pltpu.VMEM((count, value_width + 16, key_width), low_type),
            pltpu.SemaphoreType.DMA((count - 1,)),
            pltpu.SemaphoreType.DMA((count - 1,)),
        ],
        compiler_params=comm_params(collective),
        cost_estimate=pl.CostEstimate(flops=0, bytes_accessed=80_000_000, transcendentals=0),
    )(convolved, cumulative, states, grad_attended)


def halve_rows(value, order):
    count = lax.axis_size("seq")
    me = lax.axis_index("seq")
    bits = count.bit_length() - 1
    height, width = value.shape
    left = list(reversed(range(bits)))
    view = value.reshape((2,) * bits + (height // count, width))
    for bit in order(bits):
        dim = left.index(bit)
        own = (me // (1 << bit)) % 2
        sent = lax.dynamic_index_in_dim(view, 1 - own, dim, False)
        kept = lax.dynamic_index_in_dim(view, own, dim, False)
        got = lax.ppermute(
            sent.astype(low_type), "seq", [(place, place ^ (1 << bit)) for place in range(count)]
        )
        view = kept + got.astype(jnp.float32)
        left.remove(bit)
    return view


def upward(bits):
    return list(range(bits))


def near_last(bits):
    return list(range(1, bits)) + [0]


def on_device(
    tokens,
    attn_gain,
    w_in,
    conv_weight,
    gate_down,
    gate_up,
    forget_bias,
    out_gain,
    w_out,
    mlp_gain,
    w_gate_up,
    w_down,
    cotangent,
):
    tok_count = tokens.shape[0]
    qkv_width = conv_weight.shape[1]
    key_width = gate_up.shape[1]
    value_width = out_gain.shape[0]
    rim_rows = conv_weight.shape[0] - 1
    inputs = tokens.astype(jnp.float32)
    attn_gain32 = attn_gain.astype(jnp.float32)
    normed32, attn_norm_back = jax.vjp(rms_norm, inputs, attn_gain32)
    normed = normed32.astype(jnp.bfloat16)
    projected = product_plain(normed, w_in)
    mixed_pre = projected[:, :qkv_width].astype(jnp.bfloat16)
    out_gate = projected[:, qkv_width:]
    prev_rows = from_behind(mixed_pre[tok_count - rim_rows :], "seq", 1)
    extended = jnp.concatenate([prev_rows, mixed_pre], axis=0).astype(jnp.float32)
    kernel = conv_weight.astype(jnp.float32)
    conv_pre = jnp.zeros((tok_count, qkv_width), jnp.float32)
    for offset in range(rim_rows + 1):
        conv_pre = conv_pre + kernel[offset] * extended[offset : offset + tok_count]
    activated, silu_back = jax.vjp(jax.nn.silu, conv_pre)
    convolved = lax.optimization_barrier(activated.astype(jnp.bfloat16))
    low_rank = product_plain(normed, gate_down)
    gate_up32 = gate_up.astype(jnp.float32)
    logits = product_exact(low_rank, gate_up32) + forget_bias.astype(jnp.float32)
    log_decay, decay_back = jax.vjp(decay_of, logits)
    attended, cumulative, states = mixer_forward(convolved, log_decay, value_width, 1)
    out_gain32 = out_gain.astype(jnp.float32)
    gated32, gate_back = jax.vjp(gate_norm, attended, out_gain32, out_gate)
    gated = gated32.astype(jnp.bfloat16)
    mixer_total = head_sum(product_plain(gated, w_out), 2)
    residual = inputs + mixer_total
    mlp_gain32 = mlp_gain.astype(jnp.float32)
    normed_mlp32, mlp_norm_back = jax.vjp(rms_norm, residual, mlp_gain32)
    normed_mlp = normed_mlp32.astype(jnp.bfloat16)
    gate_up_val = product_plain(normed_mlp, w_gate_up)
    hidden32, act_back = jax.vjp(swiglu, gate_up_val)
    hidden = hidden32.astype(jnp.bfloat16)
    mlp_total = lax.psum(product_plain(hidden, w_down).astype(jnp.bfloat16), "head").astype(
        jnp.float32
    )
    block_out = (residual + mlp_total).astype(jnp.bfloat16)
    grad_w_down = halve_rows(product_lead(cotangent, hidden), near_last)
    grad_hidden = product_last(cotangent, w_down)
    grad_gate_up_val = act_back(grad_hidden)[0].astype(jnp.bfloat16)
    grad_w_gate_up = halve_rows(product_lead(normed_mlp, grad_gate_up_val), upward)
    normed_mlp_grad = head_sum(product_last(grad_gate_up_val, w_gate_up), 3)
    grad_resid_part, grad_mlp_gain = mlp_norm_back(normed_mlp_grad)
    grad_residual = cotangent.astype(jnp.float32) + grad_resid_part
    grad_res_low = grad_residual.astype(jnp.bfloat16)
    grad_w_out = halve_rows(product_lead(grad_res_low, gated), near_last)
    grad_gated = product_last(grad_res_low, w_out)
    grad_attended, grad_out_gain, grad_out_gate = gate_back(grad_gated)
    grad_convolved, grad_decay = mixer_backward(convolved, cumulative, states, grad_attended, 4)
    grad_conv_pre = silu_back(grad_convolved)[0]
    grad_extended = jnp.zeros((tok_count + rim_rows, qkv_width), jnp.float32)
    kernel_rows = []
    for offset in range(rim_rows + 1):
        grad_extended = grad_extended + jnp.pad(
            kernel[offset] * grad_conv_pre, ((offset, rim_rows - offset), (0, 0))
        )
        kernel_rows.append(jnp.sum(extended[offset : offset + tok_count] * grad_conv_pre, axis=0))
    grad_kernel = jnp.stack(kernel_rows, axis=0)
    next_rows = from_behind(grad_extended[:rim_rows], "seq", -1)
    grad_pre = grad_extended[rim_rows:] + jnp.pad(next_rows, ((tok_count - rim_rows, 0), (0, 0)))
    grad_projected = jnp.concatenate([grad_pre, grad_out_gate], axis=1).astype(jnp.bfloat16)
    grad_w_in = halve_rows(product_lead(normed, grad_projected), upward)
    normed_grad_part = product_last(grad_projected, w_in)
    grad_logits = decay_back(grad_decay)[0]
    grad_forget_bias = jnp.sum(grad_logits, axis=0)
    grad_gate_up = product_exact(low_rank.T, grad_logits)
    grad_low_rank = product_exact(grad_logits, gate_up32.T)
    rank = gate_down.shape[1]
    width = tokens.shape[1]
    extra = jnp.concatenate(
        [
            grad_low_rank,
            grad_out_gain[:, None],
            jnp.zeros((tok_count, 128 - rank - 1), jnp.float32),
        ],
        axis=1,
    )
    summed = head_sum(jnp.concatenate([normed_grad_part, extra], axis=1), 5)
    summed_normed = summed[:, :width]
    summed_low_rank = summed[:, width : width + rank]
    summed_out_gain = summed[:, width + rank]
    grad_gate_down = lax.dot_general(
        summed_low_rank,
        normed.astype(jnp.float32),
        (((0,), (0,)), ((), ())),
        precision=lax.Precision.HIGHEST,
    )
    total_normed = summed_normed + product_exact(summed_low_rank, gate_down.astype(jnp.float32).T)
    grad_input_part, grad_attn_gain = attn_norm_back(total_normed)
    grad_tokens = (grad_residual + grad_input_part).astype(jnp.bfloat16)
    count = lax.axis_size("seq")
    share = width // count
    for_each = jnp.concatenate(
        [grad_gate_down, grad_attn_gain[None], grad_mlp_gain[None]], axis=0
    ).reshape(rank + 2, count, share)
    for_each = jnp.swapaxes(for_each, 0, 1).reshape(count, -1)
    shared = jnp.concatenate(
        [
            grad_kernel.reshape(-1),
            grad_gate_up.reshape(-1),
            grad_forget_bias,
            summed_out_gain,
        ]
    )
    sizes = (rank * share, share, share)
    length = for_each.shape[1] + shared.shape[0]
    padded = -(-length // 1024) * 1024
    small = jnp.concatenate(
        [
            for_each,
            jnp.broadcast_to(shared, (count, shared.shape[0])),
            jnp.zeros((count, padded - length), jnp.float32),
        ],
        axis=1,
    ).reshape(count, padded // 128, 128)
    sums = seq_sum(small, 6).reshape(-1)
    places = [0]
    for size in sizes + (
        grad_kernel.size,
        grad_gate_up.size,
        grad_forget_bias.size,
        summed_out_gain.size,
    ):
        places.append(places[-1] + size)
    cut = [sums[start:end] for start, end in zip(places[:-1], places[1:])]
    return (
        block_out,
        grad_tokens,
        cut[1],
        grad_w_in,
        cut[3].reshape(grad_kernel.shape),
        cut[0].reshape(rank, share).T,
        cut[4].reshape(grad_gate_up.shape),
        cut[5],
        cut[6],
        grad_w_out.T,
        cut[2],
        grad_w_gate_up,
        grad_w_down.T,
    )


def solution(mesh):
    return jax.shard_map(
        on_device,
        mesh=mesh,
        in_specs=(
            P("seq", None),
            P(),
            P(None, "head"),
            P(None, "head"),
            P(),
            P(None, "head"),
            P("head"),
            P(),
            P("head", None),
            P(),
            P(None, "head"),
            P("head", None),
            P("seq", None),
        ),
        out_specs=(
            P("seq", None),
            P("seq", None),
            P("seq"),
            P("seq", "head"),
            P(None, "head"),
            P("seq", None),
            P(None, "head"),
            P("head"),
            P(),
            P("head", "seq"),
            P("seq"),
            P("seq", "head"),
            P("head", "seq"),
        ),
        check_vma=False,
    )
```

time: 809 us -> 277 us (0.34)
  waiting for transfers between devices: 409 us -> 56.2 us
  blocking collectives: 117 us -> 0 us
  Pallas kernels: 0 us -> 100 us
  matrix products: 103 us -> 24.2 us
  other arithmetic: 85.1 us -> 22 us
  local copies, waits for them, and re-layouts: 63.7 us -> 33.7 us
  starting transfers between devices: 6.82 us -> 25.1 us
    reduce_scatter x5 -> x0, waiting for transfers between devices: 347 us -> none  [the longest x1 114 us: on_device(): lax.psum_scatter(grad_w_gate_up, 'seq', scatter_dimension=0, tiled=True)]
    pallas_call x0 -> x6, Pallas kernels: none -> 100 us  [the longest x3 33.9 us: head_sum(): pl.pallas_call(functools.partial(head_sum_kernel, pieces), out_shape=jax....]
    all_gather x3 -> x0, blocking collectives: 72.1 us -> none  [the longest x2 51.6 us: entering(): lax.all_gather(a.astype(kind), axis)]
    dot_general x55 -> x4, matrix products: 73.4 us -> 2.93 us  [product_exact(): return jnp.dot(left, right, precision=lax.Precision.HIGHEST)]
    ppermute x0 -> x12, waiting for transfers between devices: none -> 51.7 us  [halve_rows(): lax.ppermute(sent.astype(low_type), 'seq', [(place, place ^ 1 << bit) for...]
    psum x2 -> x0, waiting for transfers between devices: 45.6 us -> none  [the longest x1 30.8 us: on_device(): lax.psum(product_last(grad_gate_up_val, w_gate_up).astype(jnp.bfloat16),...]
    unnamed x1 -> x0, blocking collectives: 37.7 us -> none
    another operation x19 -> x1, other arithmetic: 19.5 us -> 0.06 us  [the longest x12 17.9 us: span_step(): cumulative = jnp.cumsum(log_decay, axis=0)]
  transfers between devices with their start and end apart: 11 -> 15, of which waited for: 10 -> 7; matrix products, arithmetic and copies ran while one was open for 6% -> 18% of each run, Pallas kernels for 0% -> 27%
where the time goes in v1:
time: 277 us; the launch traced here: 276 us
  Pallas kernels  100 us (36%)
  waiting for transfers between devices  56.2 us (20%)
  local copies, waits for them, and re-layouts  33.7 us (12%)
  starting transfers between devices  25.1 us (9%)
  matrix products  24.2 us (9%)
  other arithmetic  22 us (8%)
  between operations  15 us (5%)
    ppermute x12, waiting for transfers between devices, halve_rows(): lax.ppermute(sent.astype(low_type), 'seq', [(place, place ^ 1 << bit) for...  51.7 us
    pallas_call x3, Pallas kernels, head_sum(): pl.pallas_call(functools.partial(head_sum_kernel, pieces), out_shape=jax....  33.9 us
    pallas_call x1, Pallas kernels, mixer_backward(): pl.pallas_call(functools.partial(mixer_backward_kernel, count), out_shape...  30.2 us
    pallas_call x1, Pallas kernels, seq_sum(): pl.pallas_call(functools.partial(seq_sum_kernel, count), out_shape=jax.Sh...  21.3 us
    ppermute x12, starting transfers between devices, halve_rows(): lax.ppermute(sent.astype(low_type), 'seq', [(place, place ^ 1 << bit) for...  18.8 us
    pallas_call x1, Pallas kernels, mixer_forward(): pl.pallas_call(functools.partial(mixer_forward_kernel, count), out_shape=...  14.8 us
    unnamed x143, local copies, waits for them, and re-layouts  10.9 us
    add x10, other arithmetic, halve_rows(): view = kept + got.astype(jnp.float32)  8.24 us
  transfers between devices with their start and end apart: 15, of which 7 were waited for; matrix products, arithmetic and copies ran while one was open for 18% of the time, Pallas kernels for 27%

profile of v1, /device:TPU:0, one launch (start us, length us, event | category | flops | bytes accessed | tf_op | source)
XLA Modules:
  0.0 276.4 jit_solution(14070722267770890585)
XLA Ops:
  7.2 1.4 fusion.9
  9.9 3.2 %fusion.70 = (bf16[256,768]{1,0:T(8,128)(2,1)S(1)}, f32[256,768]{1,0:T(8,128)}) fusion(bf16[1024,768]{1,0:T(8,128)(2,1)} %param.15, bf16[256,1024]{1,0:T(8,128)(2,1)} %param.13, f32[1024]{0:T(1024)S(1)} %convert_element_type.182, f32[256]{0:T(256)S(1)} %fusion.51), kind=kOutput, calls=%fused_computation.165 | convolution fusion | flops 403898368 | bytes 3281920 | tf_op jit(solution)/shard_map/dot_general | solution.py:31
  13.1 0.7 copy-done.27
  13.8 4.8 %collective-permute-start = (bf16[3,512]{1,0:T(4,128)(2,1)S(1)}, bf16[3,512]{1,0:T(4,128)(2,1)S(1)}, u32[]{:S(2)}, u32[]{:S(2)}) collective-permute-start(bf16[3,512]{1,0:T(4,128)(2,1)S(1)} %slice.130), channel_id=1, source_target_pairs={{0,4},{4,8},{8,12},{12,16},{16,20},{20,24},{24,28},{1,5},{5,9},{9,... | collective-permute-start | bytes 9224 | tf_op jit(solution)/shard_map/ppermute | solution.py:23
  19.1 1.0 negate_multiply_fusion
  20.1 1.0 slice.131
  22.4 1.1 multiply_convert_fusion.2
  23.6 14.8 %shard_map.228 = (f32[256,256]{1,0:T(8,128)S(1)}, f32[256,128]{1,0:T(8,128)S(1)}, f32[4,256,128]{2,1,0:T(8,128)S(1)}) custom-call(bf16[256,512]{1,0:T(8,128)(2,1)S(1)} %get-tuple-element.38.conv_ref, f32[256,128]{1,0:T(8,128)S(1)} %get-tuple-element.63.decay_ref), custom_call_target="tpu_custom_call" | custom-call | bytes 60000000 | tf_op jit(solution)/shard_map/pallas_call | solution.py:300
  38.3 0.8 copy-done.3
  39.8 1.1 multiply_convert_fusion.3
  41.2 11.0 %shard_map.229 = f32[256,1024]{1,0:T(8,128)S(1)} custom-call(f32[256,1024]{1,0:T(8,128)S(1)} %fusion.71.x_ref), custom_call_target="tpu_custom_call" | custom-call | bytes 40000000 | tf_op jit(solution)/shard_map/pallas_call | solution.py:136
  53.5 1.1 fusion.58
  55.0 2.0 fusion.46
  57.0 0.7 copy-done.34
  57.7 1.4 convolution_convert_fusion
  59.1 3.5 %convolution_bitcast_fusion = f32[1024,704]{0,1:T(8,128)} fusion(bf16[256,704]{1,0:T(8,128)(2,1)} %copy-done.34, bf16[256,1024]{1,0:T(8,128)(2,1)} %param.25), kind=kOutput, calls=%fused_computation.7 | convolution fusion | flops 369098752 | bytes 3768320 | tf_op jit(solution)/shard_map/dot_general | solution.py:35
  62.6 2.0 fusion.49.x_ref
  64.6 3.6 %fusion.48 = f32[1024,1408]{1,0:T(8,128)} fusion(f32[256,704]{1,0:T(8,128)S(1)} %copy-done.29, f32[256,704]{1,0:T(8,128)S(1)} %copy-done.28, f32[256,1024]{1,0:T(8,128)S(1)} %copy-done.10, f32[1024]{0:T(1024)S(1)} %convert_element_type.189, f32[256]{0:T(256)S(1)} %fusion.53), kind=kOutput, calls=%fused_computation.125 | convolution fusion | flops 739704832 | bytes 8262656 | tf_op jit(solution)/shard_map/dot_general | solution.py:35
  68.3 11.1 %shard_map.230 = f32[256,1024]{1,0:T(8,128)S(1)} custom-call(f32[256,1024]{1,0:T(8,128)S(1)} %copy-done.2), custom_call_target="tpu_custom_call" | custom-call | bytes 40000000 | tf_op jit(solution)/shard_map/pallas_call | solution.py:136
  79.3 0.8 multiply_reduce_fusion
  80.2 5.2 %reshape.154 = f32[2,2,2,128,704]{3,2,1,0,4:T(2,128)} reshape(f32[1024,704]{0,1:T(8,128)} %convolution_bitcast_fusion) | data formatting | bytes 5767168 | tf_op jit(solution)/shard_map/reshape | solution.py:430
  85.4 1.9 constant_dynamic-slice_fusion
  87.3 3.0 %constant_dynamic-slice_fusion.1 = f32[2,1,2,128,704]{3,2,1,0,4:T(2,128)} fusion(f32[2,2,2,128,704]{3,2,1,0,4:T(2,128)} %reshape.154, s32[]{:T(128)S(6)} %select_n.121), kind=kLoop, calls=%fused_computation.135 | loop fusion | bytes 2883588 | tf_op jit(solution)/shard_map/jit(dynamic_index_in_dim)/dynamic_slice | solution.py:435
  90.3 1.0 copy.76
  91.3 4.5 %collective-permute-start.11 = (bf16[2,2,128,704]{2,3,1,0:T(8,128)(2,1)}, bf16[2,2,128,704]{2,3,1,0:T(8,128)(2,1)}, u32[]{:S(2)}, u32[]{:S(2)}) collective-permute-start(bf16[2,2,128,704]{2,3,1,0:T(8,128)(2,1)} %bitcast.121), channel_id=1, source_target_pairs={{0,8},{4,12},{8,0},{12,4},{16,24},{20,28},{24,16},{28,20},{1,9},{5... | collective-permute-start | bytes 2162696 | tf_op jit(solution)/shard_map/ppermute | solution.py:436
  95.8 3.1 %fusion = bf16[2,2,128,1408]{3,2,0,1:T(8,128)(2,1)} fusion(f32[2,2,2,128,1408]{4,3,2,1,0:T(8,128)} %bitcast.124, s32[]{:T(128)S(6)} %select_n.118), kind=kLoop, calls=%fused_computation.12 | loop fusion | bytes 2883588 | tf_op jit(solution)/shard_map/convert_element_type | solution.py:437
  98.9 2.5 collective-permute-start.8
  102.0 4.5 %all-reduce.9.cloned.1.call-done = bf16[256,1024]{1,0:T(8,128)(2,1)} async-done(((bf16[256,1024]{1,0:T(8,128)(2,1)}), bf16[256,1024]{1,0:T(8,128)(2,1)}) %all-reduce.9.cloned.1.call-update) | async-done | bytes 524304 | tf_op jit(solution)/shard_map/psum | solution.py:503
  106.5 2.4 fusion.6
  109.0 0.9 multiply_reduce_fusion.7
  109.9 0.9 add_add_fusion.2
  110.8 30.2 %shard_map.231 = (f32[256,512]{1,0:T(8,128)S(1)}, f32[256,128]{1,0:T(8,128)S(1)}) custom-call(bf16[256,512]{1,0:T(8,128)(2,1)S(1)} %get-tuple-element.38.conv_ref, f32[256,128]{1,0:T(8,128)S(1)} %copy-done.6, f32[4,256,128]{2,1,0:T(8,128)S(1)} %copy-done.4, f32[256,256]{1,0:T(8,128)S(1)} %get-tuple-element.43.grad_ref), custom_call_target="tpu_custom_call" | custom-call | bytes 80000000 | tf_op jit(solution)/shard_map/pallas_call | solution.py:405
  141.4 0.9 fusion.44
  142.6 0.7 constant_dynamic-slice_fusion.4
  144.7 1.4 collective-permute-start.1
  146.8 0.8 copy.44
  147.6 1.0 copy.47
  148.6 1.8 copy.57
  150.4 3.8 %collective-permute-start.5 = (bf16[2,2,128,256]{2,3,1,0:T(8,128)(2,1)}, bf16[2,2,128,256]{2,3,1,0:T(8,128)(2,1)}, u32[]{:S(2)}, u32[]{:S(2)}) collective-permute-start(bf16[2,2,128,256]{2,3,1,0:T(8,128)(2,1)} %bitcast.100), channel_id=1, source_target_pairs={{0,8},{4,12},{8,0},{12,4},{16,24},{20,28},{24,16},{28,20},{1,9},{5... | collective-permute-start | bytes 786440 | tf_op jit(solution)/shard_map/ppermute | solution.py:436
  154.3 1.6 fusion.33
  156.0 1.6 concatenate.28.x_ref
  157.6 11.8 %shard_map.232 = f32[256,1152]{1,0:T(8,128)S(1)} custom-call(f32[256,1152]{1,0:T(8,128)S(1)} %concatenate.28.x_ref), custom_call_target="tpu_custom_call" | custom-call | bytes 40000000 | tf_op jit(solution)/shard_map/pallas_call | solution.py:136
  170.0 0.9 fusion.5
  171.7 1.6 copy-done.16
  173.4 1.0 fusion.13
  174.4 1.1 fusion.8
  175.6 21.3 %shard_map.233 = f32[56,128]{1,0:T(8,128)S(1)} custom-call(f32[8,56,128]{2,1,0:T(8,128)S(1)} %bitcast.123), custom_call_target="tpu_custom_call" | custom-call | bytes 20000000 | tf_op jit(solution)/shard_map/pallas_call | solution.py:193
  197.6 1.0 bitcast_add_fusion.7
  198.6 2.3 collective-permute-start.6
  201.5 5.4 %collective-permute-done.6 = bf16[2,128,256]{1,2,0:T(8,128)(2,1)S(1)} collective-permute-done((bf16[2,128,256]{1,2,0:T(8,128)(2,1)S(1)}, bf16[2,128,256]{1,2,0:T(8,128)(2,1)S(1)}, u32[]{:S(2)}, u32[]{:S(2)}) %collective-permute-start.6) | collective-permute-done | bytes 131104 | tf_op jit(solution)/shard_map/ppermute | solution.py:436
  206.9 1.0 collective-permute-start.7
  209.1 2.1 collective-permute-done.7
  211.9 1.4 bitcast_add_fusion.2
  214.0 1.3 bitcast_add_fusion.1
  215.4 2.3 collective-permute-start.3
  217.8 2.5 bitcast_add_fusion
  220.5 9.5 %collective-permute-done.12 = bf16[2,128,704]{1,2,0:T(8,128)(2,1)S(1)} collective-permute-done((bf16[2,128,704]{1,2,0:T(8,128)(2,1)S(1)}, bf16[2,128,704]{1,2,0:T(8,128)(2,1)S(1)}, u32[]{:S(2)}, u32[]{:S(2)}) %collective-permute-start.12) | collective-permute-done | bytes 360480 | tf_op jit(solution)/shard_map/ppermute | solution.py:436
  230.0 1.8 collective-permute-start.13
  231.8 5.7 %collective-permute-done.3 = bf16[2,128,768]{2,1,0:T(8,128)(2,1)S(1)} collective-permute-done((bf16[2,128,768]{2,1,0:T(8,128)(2,1)S(1)}, bf16[2,128,768]{2,1,0:T(8,128)(2,1)S(1)}, u32[]{:S(2)}, u32[]{:S(2)}) %collective-permute-start.3) | collective-permute-done | bytes 393248 | tf_op jit(solution)/shard_map/ppermute | solution.py:436
  237.7 15.0 %collective-permute-done.9 = bf16[2,128,1408]{2,1,0:T(8,128)(2,1)S(1)} collective-permute-done((bf16[2,128,1408]{2,1,0:T(8,128)(2,1)S(1)}, bf16[2,128,1408]{2,1,0:T(8,128)(2,1)S(1)}, u32[]{:S(2)}, u32[]{:S(2)}) %collective-permute-start.9) | collective-permute-done | bytes 720928 | tf_op jit(solution)/shard_map/ppermute | solution.py:436
  253.0 0.8 fusion.23
  253.8 0.8 bitcast_add_fusion.8
  254.6 14.0 %collective-permute-done.10 = bf16[128,1408]{1,0:T(8,128)(2,1)S(1)} collective-permute-done((bf16[128,1408]{1,0:T(8,128)(2,1)S(1)}, bf16[128,1408]{1,0:T(8,128)(2,1)S(1)}, u32[]{:S(2)}, u32[]{:S(2)}) %collective-permute-start.10) | collective-permute-done | bytes 360480 | tf_op jit(solution)/shard_map/ppermute | solution.py:436
  268.6 0.9 bitcast_add_fusion.6
  (206 shorter events, 15.0 us)
Async XLA Ops:
  7.2 46.3 %copy-start = (bf16[1024,1408]{1,0:T(8,128)(2,1)S(1)}, bf16[1024,1408]{1,0:T(8,128)(2,1)}, u32[]{:S(2)}) copy-start(bf16[1024,1408]{1,0:T(8,128)(2,1)} %param.23) | copy-start | bytes 8650756
  7.2 99.3 %all-reduce.9.cloned.1.call-start = ((), (), s32[]{:S(2)}) async-start(), calls=%async_computation | async-start | bytes 1048576 | tf_op jit(solution)/shard_map/psum | solution.py:503
  9.2 9.5 %copy-start.48 = (f32[256]{0:T(256)}, f32[256]{0:T(256)S(1)}, u32[]{:S(2)}) copy-start(f32[256]{0:T(256)S(1)} %fusion.51) | copy-start | bytes 3076
  9.9 8.8 %copy-start.67 = (bf16[128]{0:T(256)(128)(2,1)S(1)}, bf16[128]{0:T(256)(128)(2,1)}, u32[]{:S(2)}) copy-start(bf16[128]{0:T(256)(128)(2,1)} %param.19) | copy-start | bytes 772
  9.9 8.8 %copy-start.47 = (bf16[4,512]{1,0:T(4,128)(2,1)S(1)}, bf16[4,512]{1,0:T(4,128)(2,1)}, u32[]{:S(2)}) copy-start(bf16[4,512]{1,0:T(4,128)(2,1)} %param.16) | copy-start | bytes 12292
  9.9 8.9 %copy-start.13 = (bf16[256,1024]{1,0:T(8,128)(2,1)S(1)}, bf16[256,1024]{1,0:T(8,128)(2,1)}, u32[]{:S(2)}) copy-start(bf16[256,1024]{1,0:T(8,128)(2,1)} %param.13) | copy-start | bytes 1572868
  9.9 8.9 %copy-start.65 = (bf16[1024,16]{0,1:T(8,128)(2,1)S(1)}, bf16[1024,16]{0,1:T(8,128)(2,1)}, u32[]{:S(2)}) copy-start(bf16[1024,16]{0,1:T(8,128)(2,1)} %param.17) | copy-start | bytes 98308
  9.9 9.2 %copy-start.58 = (bf16[16,128]{1,0:T(8,128)(2,1)S(1)}, bf16[16,128]{1,0:T(8,128)(2,1)}, u32[]{:S(2)}) copy-start(bf16[16,128]{1,0:T(8,128)(2,1)} %param.18) | copy-start | bytes 12292
  13.1 8.0 %copy-start.68 = (bf16[256]{0:T(256)(128)(2,1)S(1)}, bf16[256]{0:T(256)(128)(2,1)}, u32[]{:S(2)}) copy-start(bf16[256]{0:T(256)(128)(2,1)} %param.20) | copy-start | bytes 1540
  13.1 8.6 %copy-start.62 = (bf16[1024]{0:T(1024)(128)(2,1)S(1)}, bf16[1024]{0:T(1024)(128)(2,1)}, u32[]{:S(2)}) copy-start(bf16[1024]{0:T(1024)(128)(2,1)} %param.22) | copy-start | bytes 6148
  13.8 8.5 %collective-permute-start = (bf16[3,512]{1,0:T(4,128)(2,1)S(1)}, bf16[3,512]{1,0:T(4,128)(2,1)S(1)}, u32[]{:S(2)}, u32[]{:S(2)}) collective-permute-start(bf16[3,512]{1,0:T(4,128)(2,1)S(1)} %slice.130), channel_id=1, source_target_pairs={{0,4},{4,8},{8,12},{12,16},{16,20},{20,24},{24,28},{1,5},{5,9},{9,... | collective-permute-start | bytes 9224 | tf_op jit(solution)/shard_map/ppermute | solution.py:23
  18.8 4.8 %copy-start.38 = (f32[1,512]{1,0:T(1,128)}, f32[1,512]{1,0:T(1,128)S(1)}, u32[]{:S(2)}) copy-start(f32[1,512]{1,0:T(1,128)S(1)} %get-tuple-element.58) | copy-start | bytes 6148
  18.8 4.7 %copy-start.40 = (f32[1,512]{1,0:T(1,128)}, f32[1,512]{1,0:T(1,128)S(1)}, u32[]{:S(2)}) copy-start(f32[1,512]{1,0:T(1,128)S(1)} %get-tuple-element.59) | copy-start | bytes 6148
  18.8 4.7 %copy-start.42 = (f32[1,512]{1,0:T(1,128)}, f32[1,512]{1,0:T(1,128)S(1)}, u32[]{:S(2)}) copy-start(f32[1,512]{1,0:T(1,128)S(1)} %get-tuple-element.60) | copy-start | bytes 6148
  19.1 4.4 %copy-start.45 = (f32[256,16]{0,1:T(8,128)}, f32[256,16]{0,1:T(8,128)S(1)}, u32[]{:S(2)}) copy-start(f32[256,16]{0,1:T(8,128)S(1)} %fusion.61) | copy-start | bytes 49156
  22.4 17.4 %copy-start.60 = (f32[256]{0:T(256)S(1)}, f32[256]{0:T(256)}, u32[]{:S(2)}) copy-start(f32[256]{0:T(256)} %convert_element_type.187) | copy-start | bytes 3076
  22.4 18.5 %copy-start.32 = (bf16[256,1024]{1,0:T(8,128)(2,1)S(1)}, bf16[256,1024]{1,0:T(8,128)(2,1)}, u32[]{:S(2)}) copy-start(bf16[256,1024]{1,0:T(8,128)(2,1)} %param.21) | copy-start | bytes 1572868
  39.2 13.0 %copy-start.52 = (f32[256]{0:T(256)}, f32[256]{0:T(256)S(1)}, u32[]{:S(2)}) copy-start(f32[256]{0:T(256)S(1)} %multiply_reduce_fusion.9) | copy-start | bytes 3076
  40.9 11.4 %copy-start.14 = (bf16[256,1024]{1,0:T(8,128)(2,1)S(1)}, bf16[256,1024]{1,0:T(8,128)(2,1)}, u32[]{:S(2)}) copy-start(bf16[256,1024]{1,0:T(8,128)(2,1)} %param.13) | copy-start | bytes 1572868
  53.5 1.5 copy-start.64
  59.1 3.5 %copy-start.28 = (f32[256,704]{1,0:T(8,128)S(1)}, f32[256,704]{1,0:T(8,128)}, u32[]{:S(2)}) copy-start(f32[256,704]{1,0:T(8,128)} %get-tuple-element.40) | copy-start | bytes 2162692
  59.1 3.5 %copy-start.29 = (f32[256,704]{1,0:T(8,128)S(1)}, f32[256,704]{1,0:T(8,128)}, u32[]{:S(2)}) copy-start(f32[256,704]{1,0:T(8,128)} %get-tuple-element.41) | copy-start | bytes 2162692
  62.6 2.0 copy-start.10
  64.6 3.6 %copy-start.2 = (f32[256,1024]{1,0:T(8,128)S(1)}, f32[256,1024]{1,0:T(8,128)}, u32[]{:S(2)}) copy-start(f32[256,1024]{1,0:T(8,128)} %fusion.49.x_ref) | copy-start | bytes 3145732
  68.3 11.1 %copy-start.11 = (f32[256,1024]{1,0:T(8,128)S(1)}, f32[256,1024]{1,0:T(8,128)}, u32[]{:S(2)}) copy-start(f32[256,1024]{1,0:T(8,128)} %copy-done.9) | copy-start | bytes 3145732
  91.3 10.2 %copy-start.55 = (f32[256]{0:T(256)S(1)}, f32[256]{0:T(256)}, u32[]{:S(2)}) copy-start(f32[256]{0:T(256)} %copy-done.54) | copy-start | bytes 3076
  91.3 15.2 %copy-start.12 = (f32[256,1024]{1,0:T(8,128)S(1)}, f32[256,1024]{1,0:T(8,128)}, u32[]{:S(2)}) copy-start(f32[256,1024]{1,0:T(8,128)} %copy-done.9) | copy-start | bytes 3145732
  91.3 120.7 %collective-permute-start.11 = (bf16[2,2,128,704]{2,3,1,0:T(8,128)(2,1)}, bf16[2,2,128,704]{2,3,1,0:T(8,128)(2,1)}, u32[]{:S(2)}, u32[]{:S(2)}) collective-permute-start(bf16[2,2,128,704]{2,3,1,0:T(8,128)(2,1)} %bitcast.121), channel_id=1, source_target_pairs={{0,8},{4,12},{8,0},{12,4},{16,24},{20,28},{24,16},{28,20},{1,9},{5... | collective-permute-start | bytes 2162696 | tf_op jit(solution)/shard_map/ppermute | solution.py:436
  98.9 118.8 %collective-permute-start.8 = (bf16[2,2,128,1408]{3,2,0,1:T(8,128)(2,1)}, bf16[2,2,128,1408]{3,2,0,1:T(8,128)(2,1)}, u32[]{:S(2)}, u32[]{:S(2)}) collective-permute-start(bf16[2,2,128,1408]{3,2,0,1:T(8,128)(2,1)} %fusion), channel_id=1, source_target_pairs={{0,4},{4,0},{8,12},{12,8},{16,20},{20,16},{24,28},{28,24},{1,5},{5... | collective-permute-start | bytes 4325384 | tf_op jit(solution)/shard_map/ppermute | solution.py:436
  102.0 6.9 %copy-start.22 = (f32[256,768]{1,0:T(8,128)S(1)}, f32[256,768]{1,0:T(8,128)}, u32[]{:S(2)}) copy-start(f32[256,768]{1,0:T(8,128)} %get-tuple-element.62) | copy-start | bytes 2359300
  106.5 2.4 copy-start.33
  106.5 2.4 copy-start.57
  106.5 2.4 copy-start.61
  108.9 33.3 %copy-start.18 = (f32[256,1024]{1,0:T(8,128)}, f32[256,1024]{1,0:T(8,128)S(1)}, u32[]{:S(2)}) copy-start(f32[256,1024]{1,0:T(8,128)S(1)} %get-tuple-element.45) | copy-start | bytes 3145732
  108.9 1.9 copy-start.4
  109.0 1.8 copy-start.6
  109.9 31.2 %copy-start.35 = (f32[256,128]{1,0:T(8,128)S(1)}, f32[256,128]{1,0:T(8,128)}, u32[]{:S(2)}) copy-start(f32[256,128]{1,0:T(8,128)} %get-tuple-element.64) | copy-start | bytes 393220
  109.9 31.3 %copy-start.46 = (f32[256,16]{0,1:T(8,128)S(1)}, f32[256,16]{0,1:T(8,128)}, u32[]{:S(2)}) copy-start(f32[256,16]{0,1:T(8,128)} %copy-done.45) | copy-start | bytes 49156
  109.9 31.5 %copy-start.59 = (bf16[16,128]{1,0:T(8,128)(2,1)S(1)}, bf16[16,128]{1,0:T(8,128)(2,1)}, u32[]{:S(2)}) copy-start(bf16[16,128]{1,0:T(8,128)(2,1)} %param.18) | copy-start | bytes 12292
  144.4 2.4 copy-start.63
  144.7 9.6 %copy-start.20 = (bf16[1024,768]{1,0:T(8,128)(2,1)S(1)}, bf16[1024,768]{1,0:T(8,128)(2,1)}, u32[]{:S(2)}) copy-start(bf16[1024,768]{1,0:T(8,128)(2,1)} %param.15) | copy-start | bytes 4718596
  144.7 9.6 %copy-start.26 = (bf16[256,256]{1,0:T(8,128)(2,1)S(1)}, bf16[256,256]{1,0:T(8,128)(2,1)}, u32[]{:S(2)}) copy-start(bf16[256,256]{1,0:T(8,128)(2,1)} %get-tuple-element.44) | copy-start | bytes 393220
  144.7 9.5 %collective-permute-start.1 = (f32[3,512]{1,0:T(4,128)S(1)}, f32[3,512]{1,0:T(4,128)S(1)}, u32[]{:S(2)}, u32[]{:S(2)}) collective-permute-start(f32[3,512]{1,0:T(4,128)S(1)} %pad_add_fusion.1), channel_id=1, source_target_pairs={{4,0},{8,4},{12,8},{16,12},{20,16},{24,20},{28,24},{5,1},{9,5},{13... | collective-permute-start | bytes 18440 | tf_op jit(solution)/shard_map/ppermute | solution.py:23
  150.4 47.2 %collective-permute-start.5 = (bf16[2,2,128,256]{2,3,1,0:T(8,128)(2,1)}, bf16[2,2,128,256]{2,3,1,0:T(8,128)(2,1)}, u32[]{:S(2)}, u32[]{:S(2)}) collective-permute-start(bf16[2,2,128,256]{2,3,1,0:T(8,128)(2,1)} %bitcast.100), channel_id=1, source_target_pairs={{0,8},{4,12},{8,0},{12,4},{16,24},{20,28},{24,16},{28,20},{1,9},{5... | collective-permute-start | bytes 786440 | tf_op jit(solution)/shard_map/ppermute | solution.py:436
  154.3 1.6 copy-start.30
  154.3 1.6 copy-start.31
  157.5 12.0 %copy-start.15 = (bf16[256,1024]{1,0:T(8,128)(2,1)S(1)}, bf16[256,1024]{1,0:T(8,128)(2,1)}, u32[]{:S(2)}) copy-start(bf16[256,1024]{1,0:T(8,128)(2,1)} %param.13) | copy-start | bytes 1572868
  157.5 12.0 %copy-start.49 = (f32[256]{0:T(256)S(1)}, f32[256]{0:T(256)}, u32[]{:S(2)}) copy-start(f32[256]{0:T(256)} %copy-done.48) | copy-start | bytes 3076
  157.5 12.4 %copy-start.66 = (bf16[1024,16]{0,1:T(8,128)(2,1)S(1)}, bf16[1024,16]{0,1:T(8,128)(2,1)}, u32[]{:S(2)}) copy-start(bf16[1024,16]{0,1:T(8,128)(2,1)} %param.17) | copy-start | bytes 98308
  171.6 1.7 copy-start.16
  171.7 2.7 copy-start.19
  174.3 39.2 %collective-permute-start.2 = (bf16[2,2,128,768]{3,2,0,1:T(8,128)(2,1)}, bf16[2,2,128,768]{3,2,0,1:T(8,128)(2,1)}, u32[]{:S(2)}, u32[]{:S(2)}) collective-permute-start(bf16[2,2,128,768]{3,2,0,1:T(8,128)(2,1)} %fusion.13), channel_id=1, source_target_pairs={{0,4},{4,0},{8,12},{12,8},{16,20},{20,16},{24,28},{28,24},{1,5},{5... | collective-permute-start | bytes 2359304 | tf_op jit(solution)/shard_map/ppermute | solution.py:436
  174.4 23.2 %copy-start.24 = (f32[2,1,2,128,256]{3,4,2,0,1:T(8,128)S(1)}, f32[2,1,2,128,256]{3,4,2,0,1:T(8,128)}, u32[]{:S(2)}) copy-start(f32[2,1,2,128,256]{3,4,2,0,1:T(8,128)} %copy.47) | copy-start | bytes 1572868
  175.6 36.3 %copy-start.21 = (f32[2,1,2,128,704]{3,2,1,0,4:T(2,128)S(1)}, f32[2,1,2,128,704]{3,2,1,0,4:T(2,128)}, u32[]{:S(2)}) copy-start(f32[2,1,2,128,704]{3,2,1,0,4:T(2,128)} %constant_dynamic-slice_fusion.1) | copy-start | bytes 4325380
  198.6 8.3 %collective-permute-start.6 = (bf16[2,128,256]{1,2,0:T(8,128)(2,1)S(1)}, bf16[2,128,256]{1,2,0:T(8,128)(2,1)S(1)}, u32[]{:S(2)}, u32[]{:S(2)}) collective-permute-start(bf16[2,128,256]{1,2,0:T(8,128)(2,1)S(1)} %fusion.36), channel_id=1, source_target_pairs={{0,16},{4,20},{8,24},{12,28},{16,0},{20,4},{24,8},{28,12},{1,17},{... | collective-permute-start | bytes 393224 | tf_op jit(solution)/shard_map/ppermute | solution.py:436
  206.9 4.3 %collective-permute-start.7 = (bf16[128,256]{0,1:T(8,128)(2,1)S(1)}, bf16[128,256]{0,1:T(8,128)(2,1)S(1)}, u32[]{:S(2)}, u32[]{:S(2)}) collective-permute-start(bf16[128,256]{0,1:T(8,128)(2,1)S(1)} %fusion.47), channel_id=1, source_target_pairs={{0,4},{4,0},{8,12},{12,8},{16,20},{20,16},{24,28},{28,24},{1,5},{5... | collective-permute-start | bytes 196616 | tf_op jit(solution)/shard_map/ppermute | solution.py:436
  211.9 2.1 copy-start.17
  213.4 16.5 %collective-permute-start.12 = (bf16[2,128,704]{1,2,0:T(8,128)(2,1)S(1)}, bf16[2,128,704]{1,2,0:T(8,128)(2,1)S(1)}, u32[]{:S(2)}, u32[]{:S(2)}) collective-permute-start(bf16[2,128,704]{1,2,0:T(8,128)(2,1)S(1)} %fusion.22), channel_id=1, source_target_pairs={{0,16},{4,20},{8,24},{12,28},{16,0},{20,4},{24,8},{28,12},{1,17},{... | collective-permute-start | bytes 1081352 | tf_op jit(solution)/shard_map/ppermute | solution.py:436
  215.4 22.1 %collective-permute-start.3 = (bf16[2,128,768]{2,1,0:T(8,128)(2,1)S(1)}, bf16[2,128,768]{2,1,0:T(8,128)(2,1)S(1)}, u32[]{:S(2)}, u32[]{:S(2)}) collective-permute-start(bf16[2,128,768]{2,1,0:T(8,128)(2,1)S(1)} %fusion.20), channel_id=1, source_target_pairs={{0,8},{4,12},{8,0},{12,4},{16,24},{20,28},{24,16},{28,20},{1,9},{5... | collective-permute-start | bytes 1179656 | tf_op jit(solution)/shard_map/ppermute | solution.py:436
  220.4 32.3 %collective-permute-start.9 = (bf16[2,128,1408]{2,1,0:T(8,128)(2,1)S(1)}, bf16[2,128,1408]{2,1,0:T(8,128)(2,1)S(1)}, u32[]{:S(2)}, u32[]{:S(2)}) collective-permute-start(bf16[2,128,1408]{2,1,0:T(8,128)(2,1)S(1)} %fusion.15), channel_id=1, source_target_pairs={{0,8},{4,12},{8,0},{12,4},{16,24},{20,28},{24,16},{28,20},{1,9},{5... | collective-permute-start | bytes 2162696 | tf_op jit(solution)/shard_map/ppermute | solution.py:436
  230.0 23.0 %collective-permute-start.13 = (bf16[128,704]{0,1:T(8,128)(2,1)S(1)}, bf16[128,704]{0,1:T(8,128)(2,1)S(1)}, u32[]{:S(2)}, u32[]{:S(2)}) collective-permute-start(bf16[128,704]{0,1:T(8,128)(2,1)S(1)} %fusion.35), channel_id=1, source_target_pairs={{0,4},{4,0},{8,12},{12,8},{16,20},{20,16},{24,28},{28,24},{1,5},{5... | collective-permute-start | bytes 540680 | tf_op jit(solution)/shard_map/ppermute | solution.py:436
  237.6 16.2 %collective-permute-start.4 = (bf16[128,768]{1,0:T(8,128)(2,1)S(1)}, bf16[128,768]{1,0:T(8,128)(2,1)S(1)}, u32[]{:S(2)}, u32[]{:S(2)}) collective-permute-start(bf16[128,768]{1,0:T(8,128)(2,1)S(1)} %fusion.34), channel_id=1, source_target_pairs={{0,16},{4,20},{8,24},{12,28},{16,0},{20,4},{24,8},{28,12},{1,17},{... | collective-permute-start | bytes 589832 | tf_op jit(solution)/shard_map/ppermute | solution.py:436
  252.9 15.7 %collective-permute-start.10 = (bf16[128,1408]{1,0:T(8,128)(2,1)S(1)}, bf16[128,1408]{1,0:T(8,128)(2,1)S(1)}, u32[]{:S(2)}, u32[]{:S(2)}) collective-permute-start(bf16[128,1408]{1,0:T(8,128)(2,1)S(1)} %fusion.21), channel_id=1, source_target_pairs={{0,16},{4,20},{8,24},{12,28},{16,0},{20,4},{24,8},{28,12},{1,17},{... | collective-permute-start | bytes 1081352 | tf_op jit(solution)/shard_map/ppermute | solution.py:436
  253.0 16.6 %copy-start.1 = (bf16[1024,1408]{1,0:T(8,128)(2,1)S(1)}, bf16[1024,1408]{1,0:T(8,128)(2,1)}, u32[]{:S(2)}) copy-start(bf16[1024,1408]{1,0:T(8,128)(2,1)} %param.23) | copy-start | bytes 8650756
  (20 other events, 17.5 us)
Sparse Core Ops, SparseCore 0:
  68.4 38.0 all-reduce.8

commit v2 on v1

--- a/solution.py
+++ b/solution.py
@@ -149,7 +149,7 @@
             pltpu.SemaphoreType.DMA((3, pieces)),
         ],
         compiler_params=comm_params(collective),
-        cost_estimate=pl.CostEstimate(flops=0, bytes_accessed=40_000_000, transcendentals=0),
+        cost_estimate=pl.CostEstimate(flops=0, bytes_accessed=2_000_000, transcendentals=0),
     )(value)
 
 
@@ -201,18 +201,34 @@
             pltpu.SemaphoreType.DMA((count - 1,)),
         ],
         compiler_params=comm_params(collective),
-        cost_estimate=pl.CostEstimate(flops=0, bytes_accessed=20_000_000, transcendentals=0),
+        cost_estimate=pl.CostEstimate(flops=0, bytes_accessed=2_000_000, transcendentals=0),
     )(value)
 
 
-def dot_exact(left, right, left_dim, right_dim):
+def dot_one(left, right, left_dim, right_dim):
     return lax.dot_general(
-        left,
-        right,
-        (((left_dim,), (right_dim,)), ((), ())),
-        precision=lax.Precision.HIGHEST,
-        preferred_element_type=jnp.float32,
-    )
+        left, right, (((left_dim,), (right_dim,)), ((), ())), preferred_element_type=jnp.float32
+    )
+
+
+def terms(value, count):
+    parts = []
+    for _ in range(count):
+        parts.append(value.astype(low_type))
+        value = value - parts[-1].astype(jnp.float32)
+    return parts
+
+
+def dot_exact(left, right, left_dim, right_dim, count=2):
+    lefts = [left] if left.dtype == low_type else terms(left, count)
+    rights = [right] if right.dtype == low_type else terms(right, count)
+    total = None
+    for rank in reversed(range(count)):
+        for one in range(rank + 1):
+            if one < len(lefts) and rank - one < len(rights):
+                product = dot_one(lefts[one], rights[rank - one], left_dim, right_dim)
+                total = product if total is None else total + product
+    return total
 
 
 def causal_mask(size):
@@ -250,16 +266,16 @@
     value_width = attended_ref.shape[1]
     greet("seq", seq_peers(count))
     causal = causal_mask(SPAN)
-    ones = causal.astype(jnp.float32)
+    ones = causal.astype(jnp.float32).astype(low_type)
     state = jnp.zeros((value_width, key_width), jnp.float32)
     before = jnp.zeros((1, key_width), jnp.float32)
     starts = []
     for span in range(spans):
         rows = pl.ds(span * SPAN, SPAN)
-        cumulative = dot_exact(ones, decay_ref[rows, :], 1, 0)
+        cumulative = dot_exact(ones, decay_ref[rows, :], 1, 0, 3)
         total_ref[rows, :] = cumulative
         keys = conv_ref[rows, key_width : 2 * key_width].astype(jnp.float32)
-        values = conv_ref[rows, 2 * key_width :].astype(jnp.float32)
+        values = conv_ref[rows, 2 * key_width :]
         ending = cumulative[SPAN - 1 : SPAN]
         state_ref[span] = state
         starts.append(before)
@@ -276,7 +292,7 @@
         cumulative = total_ref[rows, :]
         queries = conv_ref[rows, 0:key_width].astype(jnp.float32) * key_width ** (-0.5)
         keys = conv_ref[rows, key_width : 2 * key_width].astype(jnp.float32)
-        values = conv_ref[rows, 2 * key_width :].astype(jnp.float32)
+        values = conv_ref[rows, 2 * key_width :]
         inner = queries * jnp.exp(cumulative)
         query_in[rows, :] = inner
         scores = jnp.where(causal, dot_exact(inner, keys * jnp.exp(-cumulative), 1, 1), 0.0)
@@ -314,7 +330,7 @@
             pltpu.SemaphoreType.DMA((count - 1,)),
         ],
         compiler_params=comm_params(collective),
-        cost_estimate=pl.CostEstimate(flops=0, bytes_accessed=60_000_000, transcendentals=0),
+        cost_estimate=pl.CostEstimate(flops=0, bytes_accessed=2_000_000, transcendentals=0),
     )(convolved, log_decay)
 
 
@@ -338,7 +354,7 @@
     scale = key_width ** (-0.5)
     greet("seq", seq_peers(count))
     causal = causal_mask(SPAN)
-    ones = causal.astype(jnp.float32)
+    ones = causal.astype(jnp.float32).astype(low_type)
     state = jnp.zeros((value_width, key_width), jnp.float32)
     after = jnp.zeros((1, key_width), jnp.float32)
     ends = [None] * spans
@@ -362,7 +378,7 @@
         key_in = conv_ref[rows, key_width : 2 * key_width].astype(jnp.float32) * jnp.exp(
             -cumulative
         )
-        values = conv_ref[rows, 2 * key_width :].astype(jnp.float32)
+        values = conv_ref[rows, 2 * key_width :]
         grad = grad_ref[rows, :]
         scores = jnp.where(causal, dot_exact(inner, key_in, 1, 1), 0.0)
         grad_scores = jnp.where(causal, dot_exact(grad, values, 1, 1), 0.0)
@@ -384,7 +400,7 @@
         ending = cumulative[SPAN - 1 : SPAN]
         to_end = jnp.exp(ending - cumulative)
         key_end = conv_ref[rows, key_width : 2 * key_width].astype(jnp.float32) * to_end
-        values = conv_ref[rows, 2 * key_width :].astype(jnp.float32)
+        values = conv_ref[rows, 2 * key_width :]
         out_grad = local[span] + jnp.exp(ends[span]) * leaving
         grad_key_end = dot_exact(values, out_grad, 1, 0)
         conv_grad_ref[rows, key_width : 2 * key_width] += grad_key_end * to_end
@@ -394,7 +410,7 @@
             state_ref[span] * out_grad, axis=0, keepdims=True
         )
         decay_grad_ref[rows, :] = (
-            dot_exact(ones, decay_grad_ref[rows, :] - through, 0, 0) + end_grad
+            dot_exact(ones, decay_grad_ref[rows, :] - through, 0, 0, 3) + end_grad
         )
 
 
@@ -417,36 +433,71 @@
             pltpu.SemaphoreType.DMA((count - 1,)),
         ],
         compiler_params=comm_params(collective),
-        cost_estimate=pl.CostEstimate(flops=0, bytes_accessed=80_000_000, transcendentals=0),
+        cost_estimate=pl.CostEstimate(flops=0, bytes_accessed=2_000_000, transcendentals=0),
     )(convolved, cumulative, states, grad_attended)
 
 
-def halve_rows(value, order):
+def exchange(sent, bit):
     count = lax.axis_size("seq")
-    me = lax.axis_index("seq")
-    bits = count.bit_length() - 1
-    height, width = value.shape
-    left = list(reversed(range(bits)))
-    view = value.reshape((2,) * bits + (height // count, width))
-    for bit in order(bits):
-        dim = left.index(bit)
-        own = (me // (1 << bit)) % 2
-        sent = lax.dynamic_index_in_dim(view, 1 - own, dim, False)
-        kept = lax.dynamic_index_in_dim(view, own, dim, False)
-        got = lax.ppermute(
-            sent.astype(low_type), "seq", [(place, place ^ (1 << bit)) for place in range(count)]
-        )
-        view = kept + got.astype(jnp.float32)
-        left.remove(bit)
-    return view
-
-
-def upward(bits):
-    return list(range(bits))
-
-
-def near_last(bits):
-    return list(range(1, bits)) + [0]
+    return lax.ppermute(sent, "seq", [(place, place ^ (1 << bit)) for place in range(count)])
+
+
+def bit_of_me(bit):
+    return (lax.axis_index("seq") // (1 << bit)) % 2
+
+
+def lay_columns_kernel(places, share, x_ref, o_ref):
+    for turn, place in enumerate(places):
+        o_ref[:, turn * share : (turn + 1) * share] = x_ref[:, place * share : (place + 1) * share]
+
+
+def lay_columns(value, places, share):
+    if share % 128:
+        return jnp.concatenate([value[:, p * share : (p + 1) * share] for p in places], axis=1)
+    return pl.pallas_call(
+        functools.partial(lay_columns_kernel, places, share),
+        out_shape=jax.ShapeDtypeStruct(value.shape, value.dtype),
+        in_specs=vmem_specs(1),
+        out_specs=vmem_specs(1)[0],
+        compiler_params=pltpu.CompilerParams(vmem_limit_bytes=LIMIT),
+        cost_estimate=pl.CostEstimate(flops=0, bytes_accessed=1_000_000, transcendentals=0),
+    )(value)
+
+
+def begin(left, right, order):
+    count = lax.axis_size("seq")
+    share = left.shape[1] // count
+    places = sorted(range(count), key=lambda place: [(place >> bit) % 2 for bit in order])
+    laid = lay_columns(left, places, share)
+    half = left.shape[1] // 2
+    own = bit_of_me(order[0])
+    sent_left = lax.dynamic_slice_in_dim(laid, (1 - own) * half, half, 1)
+    kept_left = lax.dynamic_slice_in_dim(laid, own * half, half, 1)
+    return (product_lead(sent_left, right).astype(low_type), product_lead(kept_left, right))
+
+
+def split_half(total, bit):
+    half = total.shape[0] // 2
+    own = bit_of_me(bit)
+    return (
+        lax.dynamic_slice_in_dim(total, (1 - own) * half, half, 0).astype(low_type),
+        lax.dynamic_slice_in_dim(total, own * half, half, 0),
+    )
+
+
+def finish(sent, kept, order):
+    total = kept + exchange(sent, order[0]).astype(jnp.float32)
+    for bit in order[1:]:
+        sent, kept = split_half(total, bit)
+        total = kept + exchange(sent, bit).astype(jnp.float32)
+    return total
+
+
+def advance(got, kept, bit):
+    return split_half(kept + got.astype(jnp.float32), bit)
+
+
+together = lax.optimization_barrier
 
 
 def on_device(
@@ -465,6 +516,9 @@
     cotangent,
 ):
     tok_count = tokens.shape[0]
+    bits = list(range(lax.axis_size("seq").bit_length() - 1))
+    near_first = bits
+    near_last = bits[1:] + bits[:1]
     qkv_width = conv_weight.shape[1]
     key_width = gate_up.shape[1]
     value_width = out_gain.shape[0]
@@ -504,18 +558,31 @@
         jnp.float32
     )
     block_out = (residual + mlp_total).astype(jnp.bfloat16)
-    grad_w_down = halve_rows(product_lead(cotangent, hidden), near_last)
+    down_sent, down_kept = begin(cotangent, hidden, near_last)
     grad_hidden = product_last(cotangent, w_down)
     grad_gate_up_val = act_back(grad_hidden)[0].astype(jnp.bfloat16)
-    grad_w_gate_up = halve_rows(product_lead(normed_mlp, grad_gate_up_val), upward)
-    normed_mlp_grad = head_sum(product_last(grad_gate_up_val, w_gate_up), 3)
+    up_sent, up_kept = begin(normed_mlp, grad_gate_up_val, near_first)
+    normed_mlp_part, down_sent, up_sent = together(
+        (product_last(grad_gate_up_val, w_gate_up), down_sent, up_sent)
+    )
+    down_got = exchange(down_sent, near_last[0])
+    up_got = exchange(up_sent, near_first[0])
+    normed_mlp_grad = head_sum(normed_mlp_part, 3)
     grad_resid_part, grad_mlp_gain = mlp_norm_back(normed_mlp_grad)
     grad_residual = cotangent.astype(jnp.float32) + grad_resid_part
     grad_res_low = grad_residual.astype(jnp.bfloat16)
-    grad_w_out = halve_rows(product_lead(grad_res_low, gated), near_last)
+    out_sent, out_kept = begin(grad_res_low, gated, near_last)
     grad_gated = product_last(grad_res_low, w_out)
     grad_attended, grad_out_gain, grad_out_gate = gate_back(grad_gated)
+    grad_attended, out_sent = together((grad_attended, out_sent))
+    out_got = exchange(out_sent, near_last[0])
     grad_convolved, grad_decay = mixer_backward(convolved, cumulative, states, grad_attended, 4)
+    grad_convolved, grad_decay, down_got, up_got, out_got = together(
+        (grad_convolved, grad_decay, down_got, up_got, out_got)
+    )
+    down_sent, down_kept = advance(down_got, down_kept, near_last[1])
+    up_sent, up_kept = advance(up_got, up_kept, near_first[1])
+    out_sent, out_kept = advance(out_got, out_kept, near_last[1])
     grad_conv_pre = silu_back(grad_convolved)[0]
     grad_extended = jnp.zeros((tok_count + rim_rows, qkv_width), jnp.float32)
     kernel_rows = []
@@ -528,7 +595,7 @@
     next_rows = from_behind(grad_extended[:rim_rows], "seq", -1)
     grad_pre = grad_extended[rim_rows:] + jnp.pad(next_rows, ((tok_count - rim_rows, 0), (0, 0)))
     grad_projected = jnp.concatenate([grad_pre, grad_out_gate], axis=1).astype(jnp.bfloat16)
-    grad_w_in = halve_rows(product_lead(normed, grad_projected), upward)
+    in_sent, in_kept = begin(normed, grad_projected, near_first)
     normed_grad_part = product_last(grad_projected, w_in)
     grad_logits = decay_back(grad_decay)[0]
     grad_forget_bias = jnp.sum(grad_logits, axis=0)
@@ -544,7 +611,22 @@
         ],
         axis=1,
     )
-    summed = head_sum(jnp.concatenate([normed_grad_part, extra], axis=1), 5)
+    extended_part = jnp.concatenate([normed_grad_part, extra], axis=1)
+    extended_part, down_sent, up_sent, out_sent, in_sent = together(
+        (extended_part, down_sent, up_sent, out_sent, in_sent)
+    )
+    down_got = exchange(down_sent, near_last[1])
+    up_got = exchange(up_sent, near_first[1])
+    out_got = exchange(out_sent, near_last[1])
+    in_got = exchange(in_sent, near_first[0])
+    summed = head_sum(extended_part, 5)
+    summed, down_got, up_got, out_got, in_got = together(
+        (summed, down_got, up_got, out_got, in_got)
+    )
+    down_sent, down_kept = advance(down_got, down_kept, near_last[2])
+    up_sent, up_kept = advance(up_got, up_kept, near_first[2])
+    out_sent, out_kept = advance(out_got, out_kept, near_last[2])
+    in_sent, in_kept = advance(in_got, in_kept, near_first[1])
     summed_normed = summed[:, :width]
     summed_low_rank = summed[:, width : width + rank]
     summed_out_gain = summed[:, width + rank]
@@ -582,7 +664,17 @@
         ],
         axis=1,
     ).reshape(count, padded // 128, 128)
-    sums = seq_sum(small, 6).reshape(-1)
+    small, down_sent, up_sent, out_sent, in_sent = together(
+        (small, down_sent, up_sent, out_sent, in_sent)
+    )
+    grad_w_down = finish(down_sent, down_kept, near_last[2:])
+    grad_w_gate_up = finish(up_sent, up_kept, near_first[2:])
+    grad_w_out = finish(out_sent, out_kept, near_last[2:])
+    in_got = exchange(in_sent, near_first[1])
+    sums = seq_sum(small, 6)
+    sums, in_got = together((sums, in_got))
+    grad_w_in = finish(*advance(in_got, in_kept, near_first[2]), near_first[2:])
+    sums = sums.reshape(-1)
     places = [0]
     for size in sizes + (
         grad_kernel.size,

time: 277 us -> 238 us (0.86)
  waiting for transfers between devices: 56.2 us -> 8.33 us
  other arithmetic: 22 us -> 31.5 us
  starting transfers between devices: 25.1 us -> 28.8 us
  local copies, waits for them, and re-layouts: 33.7 us -> 30.4 us
    ppermute x12, waiting for transfers between devices: 51.7 us -> 8.17 us  [exchange(): lax.ppermute(sent, 'seq', [(place, place ^ 1 << bit) for place in range(c...]
    pallas_call x1, Pallas kernels: 21.3 us -> 14.2 us  [seq_sum(): pl.pallas_call(functools.partial(seq_sum_kernel, count), out_shape=jax.Sh...]
    dynamic_slice x5 -> x0, local copies, waits for them, and re-layouts: 6.65 us -> none  [the longest x3 4.06 us: halve_rows(): kept = lax.dynamic_index_in_dim(view, own, dim, False)]
    reshape x1 -> x0, local copies, waits for them, and re-layouts: 5.24 us -> none  [halve_rows(): view = value.reshape((2,) * bits + (height // count, width))]
    psum x1, waiting for transfers between devices: 4.47 us -> 0.01 us  [on_device(): lax.psum(product_plain(hidden, w_down).astype(jnp.bfloat16), 'head')]
    unnamed x143 -> x170, local copies, waits for them, and re-layouts: 10.9 us -> 14.2 us
    ppermute x12, starting transfers between devices: 18.8 us -> 22 us  [exchange(): lax.ppermute(sent, 'seq', [(place, place ^ 1 << bit) for place in range(c...]
    pallas_call x1, Pallas kernels: 30.2 us -> 33.3 us  [mixer_backward(): pl.pallas_call(functools.partial(mixer_backward_kernel, count), out_shape...]
  transfers between devices with their start and end apart: 15 -> 15, of which waited for: 7 -> 4; matrix products, arithmetic and copies ran while one was open for 18% -> 16% of each run, Pallas kernels for 27% -> 26%
where the time goes in v2:
time: 238 us; the launch traced here: 237 us
  Pallas kernels  98.2 us (41%)
  other arithmetic  31.5 us (13%)
  local copies, waits for them, and re-layouts  30.4 us (13%)
  starting transfers between devices  28.8 us (12%)
  matrix products  24.6 us (10%)
  between operations  15.1 us (6%)
  waiting for transfers between devices  8.33 us (4%)
    pallas_call x3, Pallas kernels, head_sum(): pl.pallas_call(functools.partial(head_sum_kernel, pieces), out_shape=jax....  36.3 us
    pallas_call x1, Pallas kernels, mixer_backward(): pl.pallas_call(functools.partial(mixer_backward_kernel, count), out_shape...  33.3 us
    ppermute x12, starting transfers between devices, exchange(): lax.ppermute(sent, 'seq', [(place, place ^ 1 << bit) for place in range(c...  22 us
    unnamed x170, local copies, waits for them, and re-layouts  14.2 us
    pallas_call x1, Pallas kernels, mixer_forward(): pl.pallas_call(functools.partial(mixer_forward_kernel, count), out_shape=...  14.2 us
    pallas_call x1, Pallas kernels, seq_sum(): pl.pallas_call(functools.partial(seq_sum_kernel, count), out_shape=jax.Sh...  14.2 us
    dot_general x8, matrix products, product_lead(): lax.dot_general(left, right, (((0,), (0,)), ((), ())), preferred_element_...  8.74 us
    ppermute x12, waiting for transfers between devices, exchange(): lax.ppermute(sent, 'seq', [(place, place ^ 1 << bit) for place in range(c...  8.17 us
  transfers between devices with their start and end apart: 15, of which 4 were waited for; matrix products, arithmetic and copies ran while one was open for 16% of the time, Pallas kernels for 26%

profile of v2, /device:TPU:0, one launch (start us, length us, event | category | flops | bytes accessed | tf_op | source)
XLA Modules:
  0.0 236.9 jit_solution(8282179242379280524)
XLA Ops:
  7.2 1.4 fusion.8
  9.9 1.2 fusion.3.x_ref
  11.2 1.5 fusion.68
  14.0 5.4 %collective-permute-start = (bf16[3,512]{1,0:T(4,128)(2,1)}, bf16[3,512]{1,0:T(4,128)(2,1)}, u32[]{:S(2)}, u32[]{:S(2)}) collective-permute-start(bf16[3,512]{1,0:T(4,128)(2,1)} %slice.130), channel_id=1, source_target_pairs={{0,4},{4,8},{8,12},{12,16},{16,20},{20,24},{24,28},{1,5},{5,9},{9,... | collective-permute-start | bytes 9224 | tf_op jit(solution)/shard_map/ppermute | solution.py:23
  20.9 1.0 negate_multiply_fusion
  22.0 1.9 slice.131
  23.9 1.2 convert_element_type.151
  25.8 0.8 copy-done.9
  26.6 1.0 maximum_convert_fusion
  27.7 2.0 multiply_convert_fusion.2
  29.7 14.2 %shard_map.228 = (f32[256,256]{1,0:T(8,128)S(1)}, f32[256,128]{1,0:T(8,128)S(1)}, f32[4,256,128]{2,1,0:T(8,128)S(1)}) custom-call(bf16[256,512]{1,0:T(8,128)(2,1)S(1)} %get-tuple-element.118.conv_ref, f32[256,128]{1,0:T(8,128)S(1)} %get-tuple-element.143.decay_ref), custom_call_target="tpu_custom_call" | custom-call | bytes 2000000 | tf_op jit(solution)/shard_map/pallas_call | solution.py:316
  45.7 11.0 %shard_map.229 = f32[256,1024]{1,0:T(8,128)S(1)} custom-call(f32[256,1024]{1,0:T(8,128)S(1)} %fusion.70.x_ref), custom_call_target="tpu_custom_call" | custom-call | bytes 2000000 | tf_op jit(solution)/shard_map/pallas_call | solution.py:136
  57.3 1.0 fusion.71
  59.1 0.9 fusion.46
  60.2 1.0 fusion.72.x_ref
  61.2 1.7 convolution_convert_fusion
  63.0 1.3 convolution_convert_fusion.2
  64.2 11.0 %shard_map.232 = f32[256,1024]{1,0:T(8,128)S(1)} custom-call(f32[256,1024]{1,0:T(8,128)S(1)} %fusion.72.x_ref), custom_call_target="tpu_custom_call" | custom-call | bytes 2000000 | tf_op jit(solution)/shard_map/pallas_call | solution.py:136
  75.3 0.9 multiply_reduce_fusion
  76.8 1.6 multiply_reduce_fusion.7
  78.5 0.8 copy-done.12
  79.2 1.4 copy.37
  80.7 2.8 %collective-permute-start.2 = (bf16[512,1408]{1,0:T(8,128)(2,1)}, bf16[512,1408]{1,0:T(8,128)(2,1)S(1)}, u32[]{:S(2)}, u32[]{:S(2)}) collective-permute-start(bf16[512,1408]{1,0:T(8,128)(2,1)} %convolution_convert_fusion), channel_id=1, source_target_pairs={{0,4},{4,0},{8,12},{12,8},{16,20},{20,16},{24,28},{28,24},{1,5},{5... | collective-permute-start | bytes 4325384 | tf_op jit(solution)/shard_map/ppermute | solution.py:442
  84.1 1.3 convolution_convert_fusion.4
  85.5 1.4 add_add_fusion.2
  86.9 2.6 %collective-permute-start.3 = (bf16[512,256]{1,0:T(8,128)(2,1)S(1)}, bf16[512,256]{1,0:T(8,128)(2,1)S(1)}, u32[]{:S(2)}, u32[]{:S(2)}) collective-permute-start(bf16[512,256]{1,0:T(8,128)(2,1)S(1)} %convolution_convert_fusion.4), channel_id=1, source_target_pairs={{0,8},{4,12},{8,0},{12,4},{16,24},{20,28},{24,16},{28,20},{1,9},{5... | collective-permute-start | bytes 786440 | tf_op jit(solution)/shard_map/ppermute | solution.py:442
  89.6 33.3 %shard_map.234 = (f32[256,512]{1,0:T(8,128)S(1)}, f32[256,128]{1,0:T(8,128)S(1)}) custom-call(bf16[256,512]{1,0:T(8,128)(2,1)S(1)} %copy-done.8, f32[256,128]{1,0:T(8,128)S(1)} %copy-done.23, f32[4,256,128]{2,1,0:T(8,128)S(1)} %copy-done.21, f32[256,256]{1,0:T(8,128)S(1)} %get-tuple-element.49.grad_ref), custom_call_target="tpu_custom_call" | custom-call | bytes 2000000 | tf_op jit(solution)/shard_map/pallas_call | solution.py:421
  125.6 1.2 multiply_reduce_fusion.6
  128.7 0.9 fusion.43
  129.5 1.3 collective-permute-start.4
  131.2 1.1 copy-done.37
  132.2 0.8 dynamic-slice_convert_fusion.3
  133.3 0.9 dynamic-slice_convert_fusion
  135.9 1.7 fusion.45
  137.5 1.3 convolution_convert_fusion.1
  139.5 2.3 concatenate.28.x_ref
  141.7 2.6 %collective-permute-start.8 = (bf16[512,768]{1,0:T(8,128)(2,1)}, bf16[512,768]{1,0:T(8,128)(2,1)}, u32[]{:S(2)}, u32[]{:S(2)}) collective-permute-start(bf16[512,768]{1,0:T(8,128)(2,1)} %convolution_convert_fusion.1), channel_id=1, source_target_pairs={{0,4},{4,0},{8,12},{12,8},{16,20},{20,16},{24,28},{28,24},{1,5},{5... | collective-permute-start | bytes 2359304 | tf_op jit(solution)/shard_map/ppermute | solution.py:442
  144.4 2.6 %collective-permute-start.6 = (bf16[256,1408]{1,0:T(8,128)(2,1)}, bf16[256,1408]{1,0:T(8,128)(2,1)}, u32[]{:S(2)}, u32[]{:S(2)}) collective-permute-start(bf16[256,1408]{1,0:T(8,128)(2,1)} %dynamic-slice_convert_fusion), channel_id=1, source_target_pairs={{0,8},{4,12},{8,0},{12,4},{16,24},{20,28},{24,16},{28,20},{1,9},{5... | collective-permute-start | bytes 2162696 | tf_op jit(solution)/shard_map/ppermute | solution.py:442
  147.6 2.7 %collective-permute-start.5 = (bf16[256,704]{0,1:T(8,128)(2,1)}, bf16[256,704]{0,1:T(8,128)(2,1)}, u32[]{:S(2)}, u32[]{:S(2)}) collective-permute-start(bf16[256,704]{0,1:T(8,128)(2,1)} %dynamic-slice_convert_fusion.3), channel_id=1, source_target_pairs={{0,16},{4,20},{8,24},{12,28},{16,0},{20,4},{24,8},{28,12},{1,17},{... | collective-permute-start | bytes 1081352 | tf_op jit(solution)/shard_map/ppermute | solution.py:442
  150.3 2.9 %convolution_convert_fusion.3 = bf16[256,1024]{1,0:T(8,128)(2,1)} fusion(bf16[256,704]{1,0:T(8,128)(2,1)} %copy-done.51, bf16[704,1024]{1,0:T(8,128)(2,1)} %param.24), kind=kOutput, calls=%fused_computation.16 | convolution fusion | flops 369360896 | bytes 2326528 | tf_op jit(solution)/shard_map/dot_general | solution.py:31
  154.8 0.9 convolution_bitcast_fusion.1
  155.7 1.3 copy-done.2
  157.1 14.2 %shard_map.236 = f32[256,1152]{1,0:T(8,128)S(1)} custom-call(f32[256,1152]{1,0:T(8,128)S(1)} %copy-done.2), custom_call_target="tpu_custom_call" | custom-call | bytes 2000000 | tf_op jit(solution)/shard_map/pallas_call | solution.py:136
  171.3 1.1 collective-permute-done.7
  173.7 1.8 fusion.4
  175.6 1.3 convert_add_fusion.7
  176.9 1.8 convert_add_fusion.2
  178.8 1.1 copy-done.35
  179.9 0.8 dynamic-slice_convert_fusion.1
  180.7 1.3 convert_add_fusion.3
  183.2 0.8 dynamic-slice_convert_fusion.2
  185.5 1.4 collective-permute-start.13
  186.9 2.6 %collective-permute-start.12 = (bf16[128,1408]{1,0:T(8,128)(2,1)}, bf16[128,1408]{1,0:T(8,128)(2,1)}, u32[]{:S(2)}, u32[]{:S(2)}) collective-permute-start(bf16[128,1408]{1,0:T(8,128)(2,1)} %dynamic-slice_convert_fusion.2), channel_id=1, source_target_pairs={{0,16},{4,20},{8,24},{12,28},{16,0},{20,4},{24,8},{28,12},{1,17},{... | collective-permute-start | bytes 1081352 | tf_op jit(solution)/shard_map/ppermute | solution.py:442
  189.5 1.9 collective-permute-start.9
  191.9 3.7 %fusion.7 = (bf16[256,1024]{1,0:T(8,128)(2,1)}, bf16[256,1024]{1,0:T(8,128)(2,1)}) fusion(bf16[256,1024]{1,0:T(8,128)(2,1)} %param.13, f32[256,1024]{1,0:T(8,128)} %get-tuple-element.146, f32[256]{0:T(256)} %multiply_multiply_fusion, f32[1024]{0:T(1024)S(1)} %convert_element_type.146, f32[256]{0:T(256)} %copy-done.71, f32[256,1024]{1,0:T(8,128)} %copy-done.26, ...), kind=kLoop, calls=%fused_computation.29 | loop fusion | flops 4718592 | bytes 5779456 | tf_op jit(solution)/shard_map/convert_element_type | solution.py:641
  195.7 14.2 %shard_map.237 = f32[56,128]{1,0:T(8,128)S(1)} custom-call(f32[8,56,128]{2,1,0:T(8,128)S(1)} %bitcast.71), custom_call_target="tpu_custom_call" | custom-call | bytes 2000000 | tf_op jit(solution)/shard_map/pallas_call | solution.py:193
  209.9 0.8 copy.38
  210.7 2.0 add_bitcast_fusion
  212.6 2.1 convert_add_fusion.6
  215.9 2.0 convert_add_fusion.5
  218.5 1.0 dynamic-slice_convert_fusion.4
  219.5 1.8 collective-permute-start.10
  221.9 6.3 %collective-permute-done.10 = bf16[128,768]{1,0:T(8,128)(2,1)S(1)} collective-permute-done((bf16[128,768]{1,0:T(8,128)(2,1)S(1)}, bf16[128,768]{1,0:T(8,128)(2,1)S(1)}, u32[]{:S(2)}, u32[]{:S(2)}) %collective-permute-start.10) | collective-permute-done | bytes 196640 | tf_op jit(solution)/shard_map/ppermute | solution.py:442
  228.2 1.8 convert_add_fusion.9
  (235 shorter events, 25.9 us)
Async XLA Ops:
  7.2 50.1 %copy-start = (bf16[1024,1408]{1,0:T(8,128)(2,1)S(1)}, bf16[1024,1408]{1,0:T(8,128)(2,1)}, u32[]{:S(2)}) copy-start(bf16[1024,1408]{1,0:T(8,128)(2,1)} %param.23) | copy-start | bytes 8650756
  7.2 184.7 %all-reduce.9.cloned.1.call-start = ((), (), s32[]{:S(2)}) async-start(), calls=%async_computation | async-start | bytes 1048576 | tf_op jit(solution)/shard_map/psum | solution.py:557
  7.2 3.9 %copy-start.33 = (bf16[1024,768]{1,0:T(8,128)(2,1)S(1)}, bf16[1024,768]{1,0:T(8,128)(2,1)}, u32[]{:S(2)}) copy-start(bf16[1024,768]{1,0:T(8,128)(2,1)} %param.15) | copy-start | bytes 4718596
  11.1 8.3 %copy-start.82 = (bf16[128]{0:T(256)(128)(2,1)S(1)}, bf16[128]{0:T(256)(128)(2,1)}, u32[]{:S(2)}) copy-start(bf16[128]{0:T(256)(128)(2,1)} %param.19) | copy-start | bytes 772
  11.2 8.3 %copy-start.68 = (bf16[4,512]{1,0:T(4,128)(2,1)S(1)}, bf16[4,512]{1,0:T(4,128)(2,1)}, u32[]{:S(2)}) copy-start(bf16[4,512]{1,0:T(4,128)(2,1)} %param.16) | copy-start | bytes 12292
  11.2 8.9 %copy-start.61 = (bf16[1024,16]{0,1:T(8,128)(2,1)S(1)}, bf16[1024,16]{0,1:T(8,128)(2,1)}, u32[]{:S(2)}) copy-start(bf16[1024,16]{0,1:T(8,128)(2,1)} %param.17) | copy-start | bytes 98308
  11.2 9.7 %copy-start.78 = (bf16[16,128]{1,0:T(8,128)(2,1)S(1)}, bf16[16,128]{1,0:T(8,128)(2,1)}, u32[]{:S(2)}) copy-start(bf16[16,128]{1,0:T(8,128)(2,1)} %param.18) | copy-start | bytes 12292
  14.0 12.6 %collective-permute-start = (bf16[3,512]{1,0:T(4,128)(2,1)}, bf16[3,512]{1,0:T(4,128)(2,1)}, u32[]{:S(2)}, u32[]{:S(2)}) collective-permute-start(bf16[3,512]{1,0:T(4,128)(2,1)} %slice.130), channel_id=1, source_target_pairs={{0,4},{4,8},{8,12},{12,16},{16,20},{20,24},{24,28},{1,5},{5,9},{9,... | collective-permute-start | bytes 9224 | tf_op jit(solution)/shard_map/ppermute | solution.py:23
  20.0 7.6 %copy-start.63 = (f32[1,512]{1,0:T(1,128)}, f32[1,512]{1,0:T(1,128)S(1)}, u32[]{:S(2)}) copy-start(f32[1,512]{1,0:T(1,128)S(1)} %get-tuple-element.138) | copy-start | bytes 6148
  21.9 3.9 %copy-start.3 = (bf16[256,1024]{1,0:T(8,128)(2,1)S(1)}, bf16[256,1024]{1,0:T(8,128)(2,1)}, u32[]{:S(2)}) copy-start(bf16[256,1024]{1,0:T(8,128)(2,1)} %x_ref.1) | copy-start | bytes 1572868
  22.0 3.1 %copy-start.14 = (bf16[256,1024]{1,0:T(8,128)(2,1)}, bf16[256,1024]{1,0:T(8,128)(2,1)S(1)}, u32[]{:S(2)}) copy-start(bf16[256,1024]{1,0:T(8,128)(2,1)S(1)} %shard_map.235) | copy-start | bytes 1572868
  27.6 2.1 copy-start.24
  27.7 16.4 %copy-start.43 = (f32[256,768]{1,0:T(8,128)S(1)}, f32[256,768]{1,0:T(8,128)}, u32[]{:S(2)}) copy-start(f32[256,768]{1,0:T(8,128)} %get-tuple-element.142) | copy-start | bytes 2359300
  27.7 16.4 %copy-start.80 = (f32[256]{0:T(256)S(1)}, f32[256]{0:T(256)}, u32[]{:S(2)}) copy-start(f32[256]{0:T(256)} %convert_element_type.151) | copy-start | bytes 3076
  27.7 17.7 %copy-start.57 = (bf16[256,1024]{1,0:T(8,128)(2,1)S(1)}, bf16[256,1024]{1,0:T(8,128)(2,1)}, u32[]{:S(2)}) copy-start(bf16[256,1024]{1,0:T(8,128)(2,1)} %param.21) | copy-start | bytes 1572868
  29.7 14.5 %copy-start.7 = (bf16[256,512]{1,0:T(8,128)(2,1)}, bf16[256,512]{1,0:T(8,128)(2,1)S(1)}, u32[]{:S(2)}) copy-start(bf16[256,512]{1,0:T(8,128)(2,1)S(1)} %get-tuple-element.118.conv_ref) | copy-start | bytes 786436
  43.9 32.6 %copy-start.6 = (f32[256,256]{1,0:T(8,128)}, f32[256,256]{1,0:T(8,128)S(1)}, u32[]{:S(2)}) copy-start(f32[256,256]{1,0:T(8,128)S(1)} %get-tuple-element.45) | copy-start | bytes 786436
  44.1 12.7 %copy-start.75 = (f32[256]{0:T(256)}, f32[256]{0:T(256)S(1)}, u32[]{:S(2)}) copy-start(f32[256]{0:T(256)S(1)} %multiply_reduce_fusion.9) | copy-start | bytes 3076
  44.1 32.5 %copy-start.76 = (f32[256]{0:T(256)}, f32[256]{0:T(256)S(1)}, u32[]{:S(2)}) copy-start(f32[256]{0:T(256)S(1)} %fusion.57) | copy-start | bytes 3076
  45.7 11.1 %copy-start.29 = (bf16[256,1024]{1,0:T(8,128)(2,1)S(1)}, bf16[256,1024]{1,0:T(8,128)(2,1)}, u32[]{:S(2)}) copy-start(bf16[256,1024]{1,0:T(8,128)(2,1)} %param.13) | copy-start | bytes 1572868
  57.0 19.2 %copy-start.26 = (f32[256,1024]{1,0:T(8,128)}, f32[256,1024]{1,0:T(8,128)S(1)}, u32[]{:S(2)}) copy-start(f32[256,1024]{1,0:T(8,128)S(1)} %get-tuple-element.117) | copy-start | bytes 3145732
  57.3 3.9 %copy-start.17 = (bf16[256,1024]{1,0:T(8,128)(2,1)}, bf16[256,1024]{1,0:T(8,128)(2,1)S(1)}, u32[]{:S(2)}) copy-start(bf16[256,1024]{1,0:T(8,128)(2,1)S(1)} %shard_map.231) | copy-start | bytes 1572868
  60.0 3.0 %copy-start.51 = (bf16[256,704]{1,0:T(8,128)(2,1)}, bf16[256,704]{1,0:T(8,128)(2,1)S(1)}, u32[]{:S(2)}) copy-start(bf16[256,704]{1,0:T(8,128)(2,1)S(1)} %get-tuple-element.122) | copy-start | bytes 1081348
  78.4 11.2 %copy-start.23 = (f32[256,128]{1,0:T(8,128)S(1)}, f32[256,128]{1,0:T(8,128)}, u32[]{:S(2)}) copy-start(f32[256,128]{1,0:T(8,128)} %copy-done.22) | copy-start | bytes 393220
  80.7 8.9 %copy-start.56 = (bf16[512,704]{0,1:T(8,128)(2,1)S(1)}, bf16[512,704]{0,1:T(8,128)(2,1)}, u32[]{:S(2)}) copy-start(bf16[512,704]{0,1:T(8,128)(2,1)} %convolution_convert_fusion.2) | copy-start | bytes 2162692
  80.7 9.0 %copy-start.8 = (bf16[256,512]{1,0:T(8,128)(2,1)S(1)}, bf16[256,512]{1,0:T(8,128)(2,1)}, u32[]{:S(2)}) copy-start(bf16[256,512]{1,0:T(8,128)(2,1)} %copy-done.7) | copy-start | bytes 786436
  80.7 9.0 %copy-start.21 = (f32[4,256,128]{2,1,0:T(8,128)S(1)}, f32[4,256,128]{2,1,0:T(8,128)}, u32[]{:S(2)}) copy-start(f32[4,256,128]{2,1,0:T(8,128)} %copy-done.20) | copy-start | bytes 1572868
  80.7 44.2 %collective-permute-start.2 = (bf16[512,1408]{1,0:T(8,128)(2,1)}, bf16[512,1408]{1,0:T(8,128)(2,1)S(1)}, u32[]{:S(2)}, u32[]{:S(2)}) collective-permute-start(bf16[512,1408]{1,0:T(8,128)(2,1)} %convolution_convert_fusion), channel_id=1, source_target_pairs={{0,4},{4,0},{8,12},{12,8},{16,20},{20,16},{24,28},{28,24},{1,5},{5... | collective-permute-start | bytes 4325384 | tf_op jit(solution)/shard_map/ppermute | solution.py:442
  84.1 38.8 %copy-start.13 = (bf16[256,1024]{1,0:T(8,128)(2,1)S(1)}, bf16[256,1024]{1,0:T(8,128)(2,1)}, u32[]{:S(2)}) copy-start(bf16[256,1024]{1,0:T(8,128)(2,1)} %copy-done.12) | copy-start | bytes 1572868
  84.1 38.8 %copy-start.46 = (bf16[256,256]{1,0:T(8,128)(2,1)S(1)}, bf16[256,256]{1,0:T(8,128)(2,1)}, u32[]{:S(2)}) copy-start(bf16[256,256]{1,0:T(8,128)(2,1)} %copy-done.45) | copy-start | bytes 393220
  85.5 37.8 %copy-start.18 = (bf16[256,1024]{1,0:T(8,128)(2,1)S(1)}, bf16[256,1024]{1,0:T(8,128)(2,1)}, u32[]{:S(2)}) copy-start(bf16[256,1024]{1,0:T(8,128)(2,1)} %copy-done.17) | copy-start | bytes 1572868
  85.5 37.8 %copy-start.32 = (bf16[256,1408]{1,0:T(8,128)(2,1)S(1)}, bf16[256,1408]{1,0:T(8,128)(2,1)}, u32[]{:S(2)}) copy-start(bf16[256,1408]{1,0:T(8,128)(2,1)} %copy-done.31) | copy-start | bytes 2162692
  86.9 50.6 %copy-start.47 = (bf16[256,256]{1,0:T(8,128)(2,1)}, bf16[256,256]{1,0:T(8,128)(2,1)S(1)}, u32[]{:S(2)}) copy-start(bf16[256,256]{1,0:T(8,128)(2,1)S(1)} %get-tuple-element.124) | copy-start | bytes 393220
  86.9 37.9 %collective-permute-start.3 = (bf16[512,256]{1,0:T(8,128)(2,1)S(1)}, bf16[512,256]{1,0:T(8,128)(2,1)S(1)}, u32[]{:S(2)}, u32[]{:S(2)}) collective-permute-start(bf16[512,256]{1,0:T(8,128)(2,1)S(1)} %convolution_convert_fusion.4), channel_id=1, source_target_pairs={{0,8},{4,12},{8,0},{12,4},{16,24},{20,28},{24,16},{28,20},{1,9},{5... | collective-permute-start | bytes 786440 | tf_op jit(solution)/shard_map/ppermute | solution.py:442
  89.5 35.3 %collective-permute-start.1 = (bf16[512,704]{0,1:T(8,128)(2,1)S(1)}, bf16[512,704]{0,1:T(8,128)(2,1)S(1)}, u32[]{:S(2)}, u32[]{:S(2)}) collective-permute-start(bf16[512,704]{0,1:T(8,128)(2,1)S(1)} %copy-done.56), channel_id=1, source_target_pairs={{0,8},{4,12},{8,0},{12,4},{16,24},{20,28},{24,16},{28,20},{1,9},{5... | collective-permute-start | bytes 2162696 | tf_op jit(solution)/shard_map/ppermute | solution.py:442
  129.5 5.5 %collective-permute-start.4 = (f32[3,512]{1,0:T(4,128)S(1)}, f32[3,512]{1,0:T(4,128)S(1)}, u32[]{:S(2)}, u32[]{:S(2)}) collective-permute-start(f32[3,512]{1,0:T(4,128)S(1)} %pad_add_fusion.1), channel_id=1, source_target_pairs={{4,0},{8,4},{12,8},{16,12},{20,16},{24,20},{28,24},{5,1},{9,5},{13... | collective-permute-start | bytes 18440 | tf_op jit(solution)/shard_map/ppermute | solution.py:23
  130.9 3.4 %copy-start.49 = (f32[512,256]{1,0:T(8,128)}, f32[512,256]{1,0:T(8,128)S(1)}, u32[]{:S(2)}) copy-start(f32[512,256]{1,0:T(8,128)S(1)} %convert_add_fusion.8) | copy-start | bytes 1572868
  133.3 4.2 %copy-start.27 = (f32[512,1408]{1,0:T(8,128)}, f32[512,1408]{1,0:T(8,128)S(1)}, u32[]{:S(2)}) copy-start(f32[512,1408]{1,0:T(8,128)S(1)} %convert_add_fusion) | copy-start | bytes 8650756
  133.3 2.6 %copy-start.34 = (bf16[1024,768]{1,0:T(8,128)(2,1)S(1)}, bf16[1024,768]{1,0:T(8,128)(2,1)}, u32[]{:S(2)}) copy-start(bf16[1024,768]{1,0:T(8,128)(2,1)} %param.15) | copy-start | bytes 4718596
  135.1 2.4 %copy-start.40 = (bf16[256,512]{1,0:T(8,128)(2,1)}, bf16[256,512]{1,0:T(8,128)(2,1)S(1)}, u32[]{:S(2)}) copy-start(bf16[256,512]{1,0:T(8,128)(2,1)S(1)} %fusion.15) | copy-start | bytes 786436
  141.7 31.4 %collective-permute-start.8 = (bf16[512,768]{1,0:T(8,128)(2,1)}, bf16[512,768]{1,0:T(8,128)(2,1)}, u32[]{:S(2)}, u32[]{:S(2)}) collective-permute-start(bf16[512,768]{1,0:T(8,128)(2,1)} %convolution_convert_fusion.1), channel_id=1, source_target_pairs={{0,4},{4,0},{8,12},{12,8},{16,20},{20,16},{24,28},{28,24},{1,5},{5... | collective-permute-start | bytes 2359304 | tf_op jit(solution)/shard_map/ppermute | solution.py:442
  144.4 28.8 %collective-permute-start.6 = (bf16[256,1408]{1,0:T(8,128)(2,1)}, bf16[256,1408]{1,0:T(8,128)(2,1)}, u32[]{:S(2)}, u32[]{:S(2)}) collective-permute-start(bf16[256,1408]{1,0:T(8,128)(2,1)} %dynamic-slice_convert_fusion), channel_id=1, source_target_pairs={{0,8},{4,12},{8,0},{12,4},{16,24},{20,28},{24,16},{28,20},{1,9},{5... | collective-permute-start | bytes 2162696 | tf_op jit(solution)/shard_map/ppermute | solution.py:442
  147.6 5.9 %copy-start.77 = (f32[512]{0:T(512)S(1)}, f32[512]{0:T(512)}, u32[]{:S(2)}) copy-start(f32[512]{0:T(512)} %get-tuple-element.109) | copy-start | bytes 6148
  147.6 24.8 %collective-permute-start.5 = (bf16[256,704]{0,1:T(8,128)(2,1)}, bf16[256,704]{0,1:T(8,128)(2,1)}, u32[]{:S(2)}, u32[]{:S(2)}) collective-permute-start(bf16[256,704]{0,1:T(8,128)(2,1)} %dynamic-slice_convert_fusion.3), channel_id=1, source_target_pairs={{0,16},{4,20},{8,24},{12,28},{16,0},{20,4},{24,8},{28,12},{1,17},{... | collective-permute-start | bytes 1081352 | tf_op jit(solution)/shard_map/ppermute | solution.py:442
  153.2 19.2 %collective-permute-start.7 = (bf16[256,256]{1,0:T(8,128)(2,1)}, bf16[256,256]{1,0:T(8,128)(2,1)S(1)}, u32[]{:S(2)}, u32[]{:S(2)}) collective-permute-start(bf16[256,256]{1,0:T(8,128)(2,1)} %dynamic-slice_convert_fusion.6), channel_id=1, source_target_pairs={{0,16},{4,20},{8,24},{12,28},{16,0},{20,4},{24,8},{28,12},{1,17},{... | collective-permute-start | bytes 393224 | tf_op jit(solution)/shard_map/ppermute | solution.py:442
  157.1 16.6 %copy-start.30 = (bf16[256,1024]{1,0:T(8,128)(2,1)S(1)}, bf16[256,1024]{1,0:T(8,128)(2,1)}, u32[]{:S(2)}) copy-start(bf16[256,1024]{1,0:T(8,128)(2,1)} %param.13) | copy-start | bytes 1572868
  157.1 16.6 %copy-start.62 = (bf16[1024,16]{0,1:T(8,128)(2,1)S(1)}, bf16[1024,16]{0,1:T(8,128)(2,1)}, u32[]{:S(2)}) copy-start(bf16[1024,16]{0,1:T(8,128)(2,1)} %param.17) | copy-start | bytes 98308
  157.1 16.7 %copy-start.72 = (f32[256]{0:T(256)S(1)}, f32[256]{0:T(256)}, u32[]{:S(2)}) copy-start(f32[256]{0:T(256)} %copy-done.71) | copy-start | bytes 3076
  175.6 8.5 %copy-start.54 = (f32[256,256]{1,0:T(8,128)}, f32[256,256]{1,0:T(8,128)S(1)}, u32[]{:S(2)}) copy-start(f32[256,256]{1,0:T(8,128)S(1)} %convert_add_fusion.10) | copy-start | bytes 786436
  176.9 5.1 %copy-start.42 = (f32[256,704]{0,1:T(8,128)}, f32[256,704]{0,1:T(8,128)S(1)}, u32[]{:S(2)}) copy-start(f32[256,704]{0,1:T(8,128)S(1)} %convert_add_fusion.7) | copy-start | bytes 2162692
  176.9 3.8 %copy-start.28 = (f32[512,1408]{1,0:T(8,128)S(1)}, f32[512,1408]{1,0:T(8,128)}, u32[]{:S(2)}) copy-start(f32[512,1408]{1,0:T(8,128)} %copy-done.27) | copy-start | bytes 8650756
  180.7 3.3 %copy-start.67 = (f32[1024]{0:T(1024)S(1)}, f32[1024]{0:T(1024)}, u32[]{:S(2)}) copy-start(f32[1024]{0:T(1024)} %get-tuple-element.103) | copy-start | bytes 12292
  180.7 3.3 %copy-start.59 = (f32[7168]{0:T(1024)S(1)}, f32[7168]{0:T(1024)}, u32[]{:S(2)}) copy-start(f32[7168]{0:T(1024)} %pad.35.clone) | copy-start | bytes 86020
  182.0 9.3 %copy-start.74 = (f32[256]{0:T(256)S(1)}, f32[256]{0:T(256)}, u32[]{:S(2)}) copy-start(f32[256]{0:T(256)} %copy-done.73) | copy-start | bytes 3076
  182.0 9.9 %copy-start.5 = (bf16[256,1024]{1,0:T(8,128)(2,1)S(1)}, bf16[256,1024]{1,0:T(8,128)(2,1)}, u32[]{:S(2)}) copy-start(bf16[256,1024]{1,0:T(8,128)(2,1)} %x_ref.1) | copy-start | bytes 1572868
  182.1 9.9 %copy-start.70 = (f32[256]{0:T(256)S(1)}, f32[256]{0:T(256)}, u32[]{:S(2)}) copy-start(f32[256]{0:T(256)} %copy-done.69) | copy-start | bytes 3076
  184.9 25.0 %collective-permute-start.11 = (bf16[128,256]{1,0:T(8,128)(2,1)S(1)}, bf16[128,256]{1,0:T(8,128)(2,1)S(1)}, u32[]{:S(2)}, u32[]{:S(2)}) collective-permute-start(bf16[128,256]{1,0:T(8,128)(2,1)S(1)} %dynamic-slice_convert_fusion.7), channel_id=1, source_target_pairs={{0,4},{4,0},{8,12},{12,8},{16,20},{20,16},{24,28},{28,24},{1,5},{5... | collective-permute-start | bytes 196616 | tf_op jit(solution)/shard_map/ppermute | solution.py:442
  185.5 25.2 %collective-permute-start.13 = (bf16[128,704]{0,1:T(8,128)(2,1)}, bf16[128,704]{0,1:T(8,128)(2,1)}, u32[]{:S(2)}, u32[]{:S(2)}) collective-permute-start(bf16[128,704]{0,1:T(8,128)(2,1)} %dynamic-slice_convert_fusion.5), channel_id=1, source_target_pairs={{0,4},{4,0},{8,12},{12,8},{16,20},{20,16},{24,28},{28,24},{1,5},{5... | collective-permute-start | bytes 540680 | tf_op jit(solution)/shard_map/ppermute | solution.py:442
  186.9 25.7 %collective-permute-start.12 = (bf16[128,1408]{1,0:T(8,128)(2,1)}, bf16[128,1408]{1,0:T(8,128)(2,1)}, u32[]{:S(2)}, u32[]{:S(2)}) collective-permute-start(bf16[128,1408]{1,0:T(8,128)(2,1)} %dynamic-slice_convert_fusion.2), channel_id=1, source_target_pairs={{0,16},{4,20},{8,24},{12,28},{16,0},{20,4},{24,8},{28,12},{1,17},{... | collective-permute-start | bytes 1081352 | tf_op jit(solution)/shard_map/ppermute | solution.py:442
  189.5 25.3 %collective-permute-start.9 = (bf16[256,768]{1,0:T(8,128)(2,1)}, bf16[256,768]{1,0:T(8,128)(2,1)}, u32[]{:S(2)}, u32[]{:S(2)}) collective-permute-start(bf16[256,768]{1,0:T(8,128)(2,1)} %dynamic-slice_convert_fusion.1), channel_id=1, source_target_pairs={{0,8},{4,12},{8,0},{12,4},{16,24},{20,28},{24,16},{28,20},{1,9},{5... | collective-permute-start | bytes 1179656 | tf_op jit(solution)/shard_map/ppermute | solution.py:442
  191.9 3.8 %copy-start.19 = (f32[1,8,56,128]{3,2,1,0:T(8,128)S(1)}, f32[1,8,56,128]{3,2,1,0:T(8,128)}, u32[]{:S(2)}) copy-start(f32[1,8,56,128]{3,2,1,0:T(8,128)} %copy.46) | copy-start | bytes 688132
  191.9 17.9 %copy-start.55 = (f32[256,256]{1,0:T(8,128)S(1)}, f32[256,256]{1,0:T(8,128)}, u32[]{:S(2)}) copy-start(f32[256,256]{1,0:T(8,128)} %copy-done.54) | copy-start | bytes 786436
  210.7 5.2 %copy-start.36 = (f32[512,768]{1,0:T(8,128)S(1)}, f32[512,768]{1,0:T(8,128)}, u32[]{:S(2)}) copy-start(f32[512,768]{1,0:T(8,128)} %copy-done.35) | copy-start | bytes 4718596
  219.5 8.7 %collective-permute-start.10 = (bf16[128,768]{1,0:T(8,128)(2,1)S(1)}, bf16[128,768]{1,0:T(8,128)(2,1)S(1)}, u32[]{:S(2)}, u32[]{:S(2)}) collective-permute-start(bf16[128,768]{1,0:T(8,128)(2,1)S(1)} %dynamic-slice_convert_fusion.4), channel_id=1, source_target_pairs={{0,16},{4,20},{8,24},{12,28},{16,0},{20,4},{24,8},{28,12},{1,17},{... | collective-permute-start | bytes 589832 | tf_op jit(solution)/shard_map/ppermute | solution.py:442
  (34 other events, 39.3 us)
Sparse Core Ops, SparseCore 0:
  153.3 33.4 all-reduce.8

commit v3 on v2

--- a/solution.py
+++ b/solution.py
@@ -562,27 +562,23 @@
     grad_hidden = product_last(cotangent, w_down)
     grad_gate_up_val = act_back(grad_hidden)[0].astype(jnp.bfloat16)
     up_sent, up_kept = begin(normed_mlp, grad_gate_up_val, near_first)
-    normed_mlp_part, down_sent, up_sent = together(
-        (product_last(grad_gate_up_val, w_gate_up), down_sent, up_sent)
-    )
+    normed_mlp_part, down_sent = together((product_last(grad_gate_up_val, w_gate_up), down_sent))
     down_got = exchange(down_sent, near_last[0])
-    up_got = exchange(up_sent, near_first[0])
-    normed_mlp_grad = head_sum(normed_mlp_part, 3)
+    normed_mlp_grad, down_got = together((head_sum(normed_mlp_part, 3), down_got))
+    down_sent, down_kept = advance(down_got, down_kept, near_last[1])
     grad_resid_part, grad_mlp_gain = mlp_norm_back(normed_mlp_grad)
     grad_residual = cotangent.astype(jnp.float32) + grad_resid_part
     grad_res_low = grad_residual.astype(jnp.bfloat16)
     out_sent, out_kept = begin(grad_res_low, gated, near_last)
     grad_gated = product_last(grad_res_low, w_out)
     grad_attended, grad_out_gain, grad_out_gate = gate_back(grad_gated)
-    grad_attended, out_sent = together((grad_attended, out_sent))
+    grad_convolved, grad_decay = mixer_backward(convolved, cumulative, states, grad_attended, 4)
+    grad_convolved, grad_decay, down_sent, up_sent, out_sent = together(
+        (grad_convolved, grad_decay, down_sent, up_sent, out_sent)
+    )
+    up_got = exchange(up_sent, near_first[0])
+    down_got = exchange(down_sent, near_last[1])
     out_got = exchange(out_sent, near_last[0])
-    grad_convolved, grad_decay = mixer_backward(convolved, cumulative, states, grad_attended, 4)
-    grad_convolved, grad_decay, down_got, up_got, out_got = together(
-        (grad_convolved, grad_decay, down_got, up_got, out_got)
-    )
-    down_sent, down_kept = advance(down_got, down_kept, near_last[1])
-    up_sent, up_kept = advance(up_got, up_kept, near_first[1])
-    out_sent, out_kept = advance(out_got, out_kept, near_last[1])
     grad_conv_pre = silu_back(grad_convolved)[0]
     grad_extended = jnp.zeros((tok_count + rim_rows, qkv_width), jnp.float32)
     kernel_rows = []
@@ -595,7 +591,7 @@
     next_rows = from_behind(grad_extended[:rim_rows], "seq", -1)
     grad_pre = grad_extended[rim_rows:] + jnp.pad(next_rows, ((tok_count - rim_rows, 0), (0, 0)))
     grad_projected = jnp.concatenate([grad_pre, grad_out_gate], axis=1).astype(jnp.bfloat16)
-    in_sent, in_kept = begin(normed, grad_projected, near_first)
+    in_sent, in_kept = begin(normed, grad_projected, near_last)
     normed_grad_part = product_last(grad_projected, w_in)
     grad_logits = decay_back(grad_decay)[0]
     grad_forget_bias = jnp.sum(grad_logits, axis=0)
@@ -612,21 +608,23 @@
         axis=1,
     )
     extended_part = jnp.concatenate([normed_grad_part, extra], axis=1)
+    extended_part, down_got, up_got, out_got = together(
+        (extended_part, down_got, up_got, out_got)
+    )
+    up_sent, up_kept = advance(up_got, up_kept, near_first[1])
+    down_sent, down_kept = advance(down_got, down_kept, near_last[2])
+    out_sent, out_kept = advance(out_got, out_kept, near_last[1])
     extended_part, down_sent, up_sent, out_sent, in_sent = together(
         (extended_part, down_sent, up_sent, out_sent, in_sent)
     )
-    down_got = exchange(down_sent, near_last[1])
+    in_got = exchange(in_sent, near_last[0])
     up_got = exchange(up_sent, near_first[1])
     out_got = exchange(out_sent, near_last[1])
-    in_got = exchange(in_sent, near_first[0])
     summed = head_sum(extended_part, 5)
-    summed, down_got, up_got, out_got, in_got = together(
-        (summed, down_got, up_got, out_got, in_got)
-    )
-    down_sent, down_kept = advance(down_got, down_kept, near_last[2])
+    summed, up_got, out_got, in_got = together((summed, up_got, out_got, in_got))
     up_sent, up_kept = advance(up_got, up_kept, near_first[2])
     out_sent, out_kept = advance(out_got, out_kept, near_last[2])
-    in_sent, in_kept = advance(in_got, in_kept, near_first[1])
+    in_sent, in_kept = advance(in_got, in_kept, near_last[1])
     summed_normed = summed[:, :width]
     summed_low_rank = summed[:, width : width + rank]
     summed_out_gain = summed[:, width + rank]
@@ -670,10 +668,10 @@
     grad_w_down = finish(down_sent, down_kept, near_last[2:])
     grad_w_gate_up = finish(up_sent, up_kept, near_first[2:])
     grad_w_out = finish(out_sent, out_kept, near_last[2:])
-    in_got = exchange(in_sent, near_first[1])
+    in_got = exchange(in_sent, near_last[1])
     sums = seq_sum(small, 6)
     sums, in_got = together((sums, in_got))
-    grad_w_in = finish(*advance(in_got, in_kept, near_first[2]), near_first[2:])
+    grad_w_in = finish(*advance(in_got, in_kept, near_last[2]), near_last[2:])
     sums = sums.reshape(-1)
     places = [0]
     for size in sizes + (

time: 238 us -> 261 us (1.097)
  waiting for transfers between devices: 8.33 us -> 27.3 us
  starting transfers between devices: 28.8 us -> 33.8 us
  Pallas kernels: 98.2 us -> 95 us
  matrix products: 24.6 us -> 27.6 us
    ppermute x12, waiting for transfers between devices: 8.17 us -> 27.3 us  [exchange(): lax.ppermute(sent, 'seq', [(place, place ^ 1 << bit) for place in range(c...]
    pallas_call x1, Pallas kernels: 33.3 us -> 14.9 us  [mixer_backward(): pl.pallas_call(functools.partial(mixer_backward_kernel, count), out_shape...]
    pallas_call x1, Pallas kernels: 14.2 us -> 30.4 us  [seq_sum(): pl.pallas_call(functools.partial(seq_sum_kernel, count), out_shape=jax.Sh...]
    ppermute x12, starting transfers between devices: 22 us -> 27.1 us  [exchange(): lax.ppermute(sent, 'seq', [(place, place ^ 1 << bit) for place in range(c...]
    unnamed x170 -> x120, local copies, waits for them, and re-layouts: 14.2 us -> 14.8 us
  transfers between devices with their start and end apart: 15 -> 15, of which waited for: 4 -> 7; matrix products, arithmetic and copies ran while one was open for 16% -> 18% of each run, Pallas kernels for 26% -> 21%
where the time goes in v3:
time: 261 us; the launch traced here: 260 us
  Pallas kernels  95 us (36%)
  starting transfers between devices  33.8 us (13%)
  other arithmetic  32.8 us (13%)
  local copies, waits for them, and re-layouts  28.4 us (11%)
  matrix products  27.6 us (11%)
  waiting for transfers between devices  27.3 us (10%)
  between operations  14.9 us (6%)
    pallas_call x3, Pallas kernels, head_sum(): pl.pallas_call(functools.partial(head_sum_kernel, pieces), out_shape=jax....  35.2 us
    pallas_call x1, Pallas kernels, seq_sum(): pl.pallas_call(functools.partial(seq_sum_kernel, count), out_shape=jax.Sh...  30.4 us
    ppermute x12, waiting for transfers between devices, exchange(): lax.ppermute(sent, 'seq', [(place, place ^ 1 << bit) for place in range(c...  27.3 us
    ppermute x12, starting transfers between devices, exchange(): lax.ppermute(sent, 'seq', [(place, place ^ 1 << bit) for place in range(c...  27.1 us
    pallas_call x1, Pallas kernels, mixer_backward(): pl.pallas_call(functools.partial(mixer_backward_kernel, count), out_shape...  14.9 us
    unnamed x120, local copies, waits for them, and re-layouts  14.8 us
    pallas_call x1, Pallas kernels, mixer_forward(): pl.pallas_call(functools.partial(mixer_forward_kernel, count), out_shape=...  14.3 us
    dot_general x8, matrix products, product_lead(): lax.dot_general(left, right, (((0,), (0,)), ((), ())), preferred_element_...  10.8 us
  transfers between devices with their start and end apart: 15, of which 7 were waited for; matrix products, arithmetic and copies ran while one was open for 18% of the time, Pallas kernels for 21%

profile of v3, /device:TPU:0, one launch (start us, length us, event | category | flops | bytes accessed | tf_op | source)
XLA Modules:
  0.0 259.7 jit_solution(16151185534387470840)
XLA Ops:
  7.2 1.4 fusion.8
  9.9 1.2 fusion.3.x_ref
  11.2 1.5 fusion.68
  13.3 5.4 %collective-permute-start = (bf16[3,512]{1,0:T(4,128)(2,1)}, bf16[3,512]{1,0:T(4,128)(2,1)}, u32[]{:S(2)}, u32[]{:S(2)}) collective-permute-start(bf16[3,512]{1,0:T(4,128)(2,1)} %slice.130), channel_id=1, source_target_pairs={{0,4},{4,8},{8,12},{12,16},{16,20},{20,24},{24,28},{1,5},{5,9},{9,... | collective-permute-start | bytes 9224 | tf_op jit(solution)/shard_map/ppermute | solution.py:23
  20.9 1.0 negate_multiply_fusion
  22.7 1.2 convert_element_type.151
  24.6 1.0 copy-done.3
  26.5 1.0 maximum_convert_fusion
  27.6 1.1 multiply_convert_fusion.2
  28.7 14.3 %shard_map.228 = (f32[256,256]{1,0:T(8,128)S(1)}, f32[256,128]{1,0:T(8,128)S(1)}, f32[4,256,128]{2,1,0:T(8,128)S(1)}) custom-call(bf16[256,512]{1,0:T(8,128)(2,1)S(1)} %get-tuple-element.122.conv_ref, f32[256,128]{1,0:T(8,128)S(1)} %get-tuple-element.147.decay_ref), custom_call_target="tpu_custom_call" | custom-call | bytes 2000000 | tf_op jit(solution)/shard_map/pallas_call | solution.py:316
  43.5 11.0 %shard_map.229 = f32[256,1024]{1,0:T(8,128)S(1)} custom-call(f32[256,1024]{1,0:T(8,128)S(1)} %fusion.70.x_ref), custom_call_target="tpu_custom_call" | custom-call | bytes 2000000 | tf_op jit(solution)/shard_map/pallas_call | solution.py:136
  55.0 1.0 fusion.71
  57.8 1.0 fusion.72.x_ref
  59.2 3.6 %collective-permute-start.1 = (bf16[512,704]{0,1:T(8,128)(2,1)S(1)}, bf16[512,704]{0,1:T(8,128)(2,1)S(1)}, u32[]{:S(2)}, u32[]{:S(2)}) collective-permute-start(bf16[512,704]{0,1:T(8,128)(2,1)S(1)} %convolution_convert_fusion.2), channel_id=1, source_target_pairs={{0,8},{4,12},{8,0},{12,4},{16,24},{20,28},{24,16},{28,20},{1,9},{5... | collective-permute-start | bytes 2162696 | tf_op jit(solution)/shard_map/ppermute | solution.py:442
  63.3 11.0 %shard_map.231 = f32[256,1024]{1,0:T(8,128)S(1)} custom-call(f32[256,1024]{1,0:T(8,128)S(1)} %fusion.72.x_ref), custom_call_target="tpu_custom_call" | custom-call | bytes 2000000 | tf_op jit(solution)/shard_map/pallas_call | solution.py:136
  74.4 1.7 convolution_convert_fusion
  76.1 2.1 fusion.26
  78.2 1.2 collective-permute-done.1
  81.2 0.9 multiply_reduce_fusion.7
  82.1 1.0 convolution_convert_fusion.4
  84.8 14.9 %shard_map.232 = (f32[256,512]{1,0:T(8,128)S(1)}, f32[256,128]{1,0:T(8,128)S(1)}) custom-call(bf16[256,512]{1,0:T(8,128)(2,1)S(1)} %get-tuple-element.122.conv_ref, f32[256,128]{1,0:T(8,128)S(1)} %get-tuple-element.51.total_ref, f32[4,256,128]{2,1,0:T(8,128)S(1)} %get-tuple-element.52.state_ref, f32[256,256]{1,0:T(8,128)S(1)} %get-tuple-element.127.grad_ref), custom_call_target="tpu_custom_call" | custom-call | bytes 2000000 | tf_op jit(solution)/shard_map/pallas_call | solution.py:421
  99.7 1.0 multiply_reduce_fusion.6
  101.8 1.3 collective-permute-start.2
  103.1 3.3 %collective-permute-start.4 = (bf16[512,1408]{1,0:T(8,128)(2,1)}, bf16[512,1408]{1,0:T(8,128)(2,1)}, u32[]{:S(2)}, u32[]{:S(2)}) collective-permute-start(bf16[512,1408]{1,0:T(8,128)(2,1)} %convolution_convert_fusion), channel_id=1, source_target_pairs={{0,4},{4,0},{8,12},{12,8},{16,20},{20,16},{24,28},{28,24},{1,5},{5... | collective-permute-start | bytes 4325384 | tf_op jit(solution)/shard_map/ppermute | solution.py:442
  108.0 1.1 fusion.24
  109.0 1.0 pad_add_fusion
  110.9 4.3 %collective-permute-start.3 = (bf16[256,704]{0,1:T(8,128)(2,1)}, bf16[256,704]{0,1:T(8,128)(2,1)}, u32[]{:S(2)}, u32[]{:S(2)}) collective-permute-start(bf16[256,704]{0,1:T(8,128)(2,1)} %dynamic-slice_convert_fusion.3), channel_id=1, source_target_pairs={{0,16},{4,20},{8,24},{12,28},{16,0},{20,4},{24,8},{28,12},{1,17},{... | collective-permute-start | bytes 1081352 | tf_op jit(solution)/shard_map/ppermute | solution.py:442
  115.2 1.9 collective-permute-start.5
  117.1 1.1 fusion.15
  118.2 3.1 %fusion.45 = f32[256,1024]{1,0:T(8,128)} fusion(bf16[1024,768]{1,0:T(8,128)(2,1)} %param.15, bf16[256,256]{1,0:T(8,128)(2,1)S(1)} %get-tuple-element.128, bf16[256,512]{1,0:T(8,128)(2,1)S(1)} %fusion.15), kind=kOutput, calls=%fused_computation.116 | convolution fusion | flops 403439616 | bytes 3014656 | tf_op jit(solution)/shard_map/dot_general | solution.py:41
  122.0 2.3 concatenate.28.x_ref
  124.3 2.4 convolution_convert_fusion.1
  126.7 2.0 collective-permute-done.5
  128.7 2.8 %collective-permute-done.3 = bf16[256,704]{0,1:T(8,128)(2,1)} collective-permute-done((bf16[256,704]{0,1:T(8,128)(2,1)}, bf16[256,704]{0,1:T(8,128)(2,1)}, u32[]{:S(2)}, u32[]{:S(2)}) %collective-permute-start.3) | collective-permute-done | bytes 360480 | tf_op jit(solution)/shard_map/ppermute | solution.py:442
  131.5 7.0 %collective-permute-done.4 = bf16[512,1408]{1,0:T(8,128)(2,1)} collective-permute-done((bf16[512,1408]{1,0:T(8,128)(2,1)}, bf16[512,1408]{1,0:T(8,128)(2,1)}, u32[]{:S(2)}, u32[]{:S(2)}) %collective-permute-start.4) | collective-permute-done | bytes 1441824 | tf_op jit(solution)/shard_map/ppermute | solution.py:442
  138.4 1.3 convert_add_fusion.8
  141.2 1.1 convert_add_fusion.7
  142.3 0.9 copy-done.26
  143.9 1.7 convert_add_fusion
  145.6 1.5 copy-done.13
  147.2 0.9 dynamic-slice_convert_fusion
  148.1 3.5 %collective-permute-start.8 = (bf16[512,768]{1,0:T(8,128)(2,1)}, bf16[512,768]{1,0:T(8,128)(2,1)}, u32[]{:S(2)}, u32[]{:S(2)}) collective-permute-start(bf16[512,768]{1,0:T(8,128)(2,1)} %convolution_convert_fusion.1), channel_id=1, source_target_pairs={{0,8},{4,12},{8,0},{12,4},{16,24},{20,28},{24,16},{28,20},{1,9},{5... | collective-permute-start | bytes 2359304 | tf_op jit(solution)/shard_map/ppermute | solution.py:442
  152.3 2.9 %convolution_convert_fusion.3 = bf16[256,1024]{1,0:T(8,128)(2,1)} fusion(bf16[256,704]{1,0:T(8,128)(2,1)} %copy-done.30, bf16[704,1024]{1,0:T(8,128)(2,1)} %param.24), kind=kOutput, calls=%fused_computation.16 | convolution fusion | flops 369360896 | bytes 2326528 | tf_op jit(solution)/shard_map/dot_general | solution.py:31
  155.2 4.3 %collective-permute-start.7 = (bf16[256,256]{1,0:T(8,128)(2,1)}, bf16[256,256]{1,0:T(8,128)(2,1)S(1)}, u32[]{:S(2)}, u32[]{:S(2)}) collective-permute-start(bf16[256,256]{1,0:T(8,128)(2,1)} %dynamic-slice_convert_fusion.6), channel_id=1, source_target_pairs={{0,16},{4,20},{8,24},{12,28},{16,0},{20,4},{24,8},{28,12},{1,17},{... | collective-permute-start | bytes 393224 | tf_op jit(solution)/shard_map/ppermute | solution.py:442
  160.9 1.1 convolution_bitcast_fusion.1
  162.0 1.3 copy-done.2
  163.3 13.1 %shard_map.236 = f32[256,1152]{1,0:T(8,128)S(1)} custom-call(f32[256,1152]{1,0:T(8,128)S(1)} %copy-done.2), custom_call_target="tpu_custom_call" | custom-call | bytes 2000000 | tf_op jit(solution)/shard_map/pallas_call | solution.py:136
  176.5 10.1 %collective-permute-done.7 = bf16[256,256]{1,0:T(8,128)(2,1)S(1)} collective-permute-done((bf16[256,256]{1,0:T(8,128)(2,1)}, bf16[256,256]{1,0:T(8,128)(2,1)S(1)}, u32[]{:S(2)}, u32[]{:S(2)}) %collective-permute-start.7) | collective-permute-done | bytes 131104 | tf_op jit(solution)/shard_map/ppermute | solution.py:442
  187.4 1.8 fusion.4
  189.8 1.7 convert_add_fusion.2
  191.6 1.2 copy-done.18
  193.5 1.3 convert_add_fusion.3
  194.8 1.1 copy-done.22
  197.6 2.5 collective-permute-start.9
  200.1 1.6 collective-permute-start.11
  203.1 3.7 %fusion.7 = (bf16[256,1024]{1,0:T(8,128)(2,1)}, bf16[256,1024]{1,0:T(8,128)(2,1)}) fusion(bf16[256,1024]{1,0:T(8,128)(2,1)} %param.13, f32[256,1024]{1,0:T(8,128)} %get-tuple-element.150, f32[256]{0:T(256)} %multiply_multiply_fusion, f32[1024]{0:T(1024)S(1)} %convert_element_type.146, f32[256]{0:T(256)} %copy-done.48, f32[256,1024]{1,0:T(8,128)} %copy-done.11, ...), kind=kLoop, calls=%fused_computation.29 | loop fusion | flops 4718592 | bytes 5779456 | tf_op jit(solution)/shard_map/convert_element_type | solution.py:639
  206.9 30.4 %shard_map.237 = f32[56,128]{1,0:T(8,128)S(1)} custom-call(f32[8,56,128]{2,1,0:T(8,128)S(1)} %bitcast.71), custom_call_target="tpu_custom_call" | custom-call | bytes 2000000 | tf_op jit(solution)/shard_map/pallas_call | solution.py:193
  238.1 2.0 add_bitcast_fusion
  240.1 2.1 convert_add_fusion.6
  243.3 1.1 convert_add_fusion.5
  244.4 0.9 copy-done.25
  245.3 1.1 collective-permute-start.10
  247.6 3.5 %collective-permute-done.10 = bf16[128,768]{1,0:T(8,128)(2,1)S(1)} collective-permute-done((bf16[128,768]{1,0:T(8,128)(2,1)S(1)}, bf16[128,768]{1,0:T(8,128)(2,1)S(1)}, u32[]{:S(2)}, u32[]{:S(2)}) %collective-permute-start.10) | collective-permute-done | bytes 196640 | tf_op jit(solution)/shard_map/ppermute | solution.py:442
  251.1 1.8 convert_add_fusion.9
  (185 shorter events, 29.9 us)
Async XLA Ops:
  7.2 47.8 %copy-start = (bf16[1024,1408]{1,0:T(8,128)(2,1)S(1)}, bf16[1024,1408]{1,0:T(8,128)(2,1)}, u32[]{:S(2)}) copy-start(bf16[1024,1408]{1,0:T(8,128)(2,1)} %param.23) | copy-start | bytes 8650756
  7.2 195.9 %all-reduce.9.cloned.1.call-start = ((), (), s32[]{:S(2)}) async-start(), calls=%async_computation | async-start | bytes 1048576 | tf_op jit(solution)/shard_map/psum | solution.py:557
  7.2 3.9 %copy-start.17 = (bf16[1024,768]{1,0:T(8,128)(2,1)S(1)}, bf16[1024,768]{1,0:T(8,128)(2,1)}, u32[]{:S(2)}) copy-start(bf16[1024,768]{1,0:T(8,128)(2,1)} %param.15) | copy-start | bytes 4718596
  11.2 8.3 %copy-start.45 = (bf16[4,512]{1,0:T(4,128)(2,1)S(1)}, bf16[4,512]{1,0:T(4,128)(2,1)}, u32[]{:S(2)}) copy-start(bf16[4,512]{1,0:T(4,128)(2,1)} %param.16) | copy-start | bytes 12292
  11.2 8.8 %copy-start.57 = (bf16[128]{0:T(256)(128)(2,1)S(1)}, bf16[128]{0:T(256)(128)(2,1)}, u32[]{:S(2)}) copy-start(bf16[128]{0:T(256)(128)(2,1)} %param.19) | copy-start | bytes 772
  11.2 8.8 %copy-start.38 = (bf16[1024,16]{0,1:T(8,128)(2,1)S(1)}, bf16[1024,16]{0,1:T(8,128)(2,1)}, u32[]{:S(2)}) copy-start(bf16[1024,16]{0,1:T(8,128)(2,1)} %param.17) | copy-start | bytes 98308
  11.2 9.7 %copy-start.52 = (bf16[16,128]{1,0:T(8,128)(2,1)S(1)}, bf16[16,128]{1,0:T(8,128)(2,1)}, u32[]{:S(2)}) copy-start(bf16[16,128]{1,0:T(8,128)(2,1)} %param.18) | copy-start | bytes 12292
  13.3 13.2 %collective-permute-start = (bf16[3,512]{1,0:T(4,128)(2,1)}, bf16[3,512]{1,0:T(4,128)(2,1)}, u32[]{:S(2)}, u32[]{:S(2)}) collective-permute-start(bf16[3,512]{1,0:T(4,128)(2,1)} %slice.130), channel_id=1, source_target_pairs={{0,4},{4,8},{8,12},{12,16},{16,20},{20,24},{24,28},{1,5},{5,9},{9,... | collective-permute-start | bytes 9224 | tf_op jit(solution)/shard_map/ppermute | solution.py:23
  20.0 7.5 %copy-start.40 = (f32[1,512]{1,0:T(1,128)}, f32[1,512]{1,0:T(1,128)S(1)}, u32[]{:S(2)}) copy-start(f32[1,512]{1,0:T(1,128)S(1)} %get-tuple-element.142) | copy-start | bytes 6148
  24.6 1.0 copy-start.3
  27.5 15.6 %copy-start.27 = (f32[256,768]{1,0:T(8,128)S(1)}, f32[256,768]{1,0:T(8,128)}, u32[]{:S(2)}) copy-start(f32[256,768]{1,0:T(8,128)} %get-tuple-element.146) | copy-start | bytes 2359300
  27.5 15.6 %copy-start.54 = (f32[256]{0:T(256)S(1)}, f32[256]{0:T(256)}, u32[]{:S(2)}) copy-start(f32[256]{0:T(256)} %convert_element_type.151) | copy-start | bytes 3076
  27.5 15.7 %copy-start.34 = (bf16[256,1024]{1,0:T(8,128)(2,1)S(1)}, bf16[256,1024]{1,0:T(8,128)(2,1)}, u32[]{:S(2)}) copy-start(bf16[256,1024]{1,0:T(8,128)(2,1)} %param.21) | copy-start | bytes 1572868
  43.5 11.1 %copy-start.15 = (bf16[256,1024]{1,0:T(8,128)(2,1)S(1)}, bf16[256,1024]{1,0:T(8,128)(2,1)}, u32[]{:S(2)}) copy-start(bf16[256,1024]{1,0:T(8,128)(2,1)} %param.13) | copy-start | bytes 1572868
  54.8 25.5 %copy-start.11 = (f32[256,1024]{1,0:T(8,128)}, f32[256,1024]{1,0:T(8,128)S(1)}, u32[]{:S(2)}) copy-start(f32[256,1024]{1,0:T(8,128)S(1)} %get-tuple-element.121) | copy-start | bytes 3145732
  55.0 1.2 copy-start.4
  55.0 1.7 copy-start.56
  57.5 5.3 %copy-start.30 = (bf16[256,704]{1,0:T(8,128)(2,1)}, bf16[256,704]{1,0:T(8,128)(2,1)S(1)}, u32[]{:S(2)}) copy-start(bf16[256,704]{1,0:T(8,128)(2,1)S(1)} %get-tuple-element.126) | copy-start | bytes 1081348
  57.7 1.0 copy-start.7
  59.2 20.3 %collective-permute-start.1 = (bf16[512,704]{0,1:T(8,128)(2,1)S(1)}, bf16[512,704]{0,1:T(8,128)(2,1)S(1)}, u32[]{:S(2)}, u32[]{:S(2)}) collective-permute-start(bf16[512,704]{0,1:T(8,128)(2,1)S(1)} %convolution_convert_fusion.2), channel_id=1, source_target_pairs={{0,8},{4,12},{8,0},{12,4},{16,24},{20,28},{24,16},{28,20},{1,9},{5... | collective-permute-start | bytes 2162696 | tf_op jit(solution)/shard_map/ppermute | solution.py:442
  74.4 6.0 %copy-start.1 = (f32[256,1024]{1,0:T(8,128)}, f32[256,1024]{1,0:T(8,128)S(1)}, u32[]{:S(2)}) copy-start(f32[256,1024]{1,0:T(8,128)S(1)} %shard_map.231) | copy-start | bytes 3145732
  83.6 1.2 copy-start.20
  99.7 1.1 copy-start.41
  99.7 1.1 copy-start.42
  99.7 1.1 copy-start.43
  101.2 5.2 %copy-start.35 = (f32[256,128]{1,0:T(8,128)S(1)}, f32[256,128]{1,0:T(8,128)}, u32[]{:S(2)}) copy-start(f32[256,128]{1,0:T(8,128)} %get-tuple-element.148) | copy-start | bytes 393220
  101.2 5.9 %copy-start.53 = (bf16[16,128]{1,0:T(8,128)(2,1)S(1)}, bf16[16,128]{1,0:T(8,128)(2,1)}, u32[]{:S(2)}) copy-start(bf16[16,128]{1,0:T(8,128)(2,1)} %param.18) | copy-start | bytes 12292
  101.8 15.2 %collective-permute-start.2 = (f32[3,512]{1,0:T(4,128)}, f32[3,512]{1,0:T(4,128)}, u32[]{:S(2)}, u32[]{:S(2)}) collective-permute-start(f32[3,512]{1,0:T(4,128)} %pad_add_fusion.1), channel_id=1, source_target_pairs={{4,0},{8,4},{12,8},{16,12},{20,16},{24,20},{28,24},{5,1},{9,5},{13... | collective-permute-start | bytes 18440 | tf_op jit(solution)/shard_map/ppermute | solution.py:23
  103.1 35.3 %collective-permute-start.4 = (bf16[512,1408]{1,0:T(8,128)(2,1)}, bf16[512,1408]{1,0:T(8,128)(2,1)}, u32[]{:S(2)}, u32[]{:S(2)}) collective-permute-start(bf16[512,1408]{1,0:T(8,128)(2,1)} %convolution_convert_fusion), channel_id=1, source_target_pairs={{0,4},{4,0},{8,12},{12,8},{16,20},{20,16},{24,28},{28,24},{1,5},{5... | collective-permute-start | bytes 4325384 | tf_op jit(solution)/shard_map/ppermute | solution.py:442
  107.1 3.0 %copy-start.31 = (f32[256,128]{1,0:T(8,128)}, f32[256,128]{1,0:T(8,128)S(1)}, u32[]{:S(2)}) copy-start(f32[256,128]{1,0:T(8,128)S(1)} %get-tuple-element.119) | copy-start | bytes 393220
  109.0 1.1 copy-start.55
  110.9 20.6 %collective-permute-start.3 = (bf16[256,704]{0,1:T(8,128)(2,1)}, bf16[256,704]{0,1:T(8,128)(2,1)}, u32[]{:S(2)}, u32[]{:S(2)}) collective-permute-start(bf16[256,704]{0,1:T(8,128)(2,1)} %dynamic-slice_convert_fusion.3), channel_id=1, source_target_pairs={{0,16},{4,20},{8,24},{12,28},{16,0},{20,4},{24,8},{28,12},{1,17},{... | collective-permute-start | bytes 1081352 | tf_op jit(solution)/shard_map/ppermute | solution.py:442
  115.2 13.5 %collective-permute-start.5 = (bf16[512,256]{1,0:T(8,128)(2,1)}, bf16[512,256]{1,0:T(8,128)(2,1)}, u32[]{:S(2)}, u32[]{:S(2)}) collective-permute-start(bf16[512,256]{1,0:T(8,128)(2,1)} %convolution_convert_fusion.4), channel_id=1, source_target_pairs={{0,8},{4,12},{8,0},{12,4},{16,24},{20,28},{24,16},{28,20},{1,9},{5... | collective-permute-start | bytes 786440 | tf_op jit(solution)/shard_map/ppermute | solution.py:442
  118.2 3.1 %copy-start.23 = (bf16[256,512]{1,0:T(8,128)(2,1)}, bf16[256,512]{1,0:T(8,128)(2,1)S(1)}, u32[]{:S(2)}) copy-start(bf16[256,512]{1,0:T(8,128)(2,1)S(1)} %fusion.15) | copy-start | bytes 786436
  124.3 16.9 %copy-start.21 = (f32[512,704]{0,1:T(8,128)S(1)}, f32[512,704]{0,1:T(8,128)}, u32[]{:S(2)}) copy-start(f32[512,704]{0,1:T(8,128)} %copy-done.20) | copy-start | bytes 4325380
  138.4 5.5 %copy-start.12 = (f32[512,1408]{1,0:T(8,128)S(1)}, f32[512,1408]{1,0:T(8,128)}, u32[]{:S(2)}) copy-start(f32[512,1408]{1,0:T(8,128)} %fusion.26) | copy-start | bytes 8650756
  145.6 1.6 copy-start.13
  148.1 39.2 %collective-permute-start.8 = (bf16[512,768]{1,0:T(8,128)(2,1)}, bf16[512,768]{1,0:T(8,128)(2,1)}, u32[]{:S(2)}, u32[]{:S(2)}) collective-permute-start(bf16[512,768]{1,0:T(8,128)(2,1)} %convolution_convert_fusion.1), channel_id=1, source_target_pairs={{0,8},{4,12},{8,0},{12,4},{16,24},{20,28},{24,16},{28,20},{1,9},{5... | collective-permute-start | bytes 2359304 | tf_op jit(solution)/shard_map/ppermute | solution.py:442
  151.6 35.7 %collective-permute-start.6 = (bf16[256,1408]{1,0:T(8,128)(2,1)}, bf16[256,1408]{1,0:T(8,128)(2,1)}, u32[]{:S(2)}, u32[]{:S(2)}) collective-permute-start(bf16[256,1408]{1,0:T(8,128)(2,1)} %dynamic-slice_convert_fusion), channel_id=1, source_target_pairs={{0,8},{4,12},{8,0},{12,4},{16,24},{20,28},{24,16},{28,20},{1,9},{5... | collective-permute-start | bytes 2162696 | tf_op jit(solution)/shard_map/ppermute | solution.py:442
  155.1 32.2 %copy-start.49 = (f32[256]{0:T(256)S(1)}, f32[256]{0:T(256)}, u32[]{:S(2)}) copy-start(f32[256]{0:T(256)} %copy-done.48) | copy-start | bytes 3076
  155.2 32.2 %copy-start.39 = (bf16[1024,16]{0,1:T(8,128)(2,1)S(1)}, bf16[1024,16]{0,1:T(8,128)(2,1)}, u32[]{:S(2)}) copy-start(bf16[1024,16]{0,1:T(8,128)(2,1)} %param.17) | copy-start | bytes 98308
  155.2 31.4 %collective-permute-start.7 = (bf16[256,256]{1,0:T(8,128)(2,1)}, bf16[256,256]{1,0:T(8,128)(2,1)S(1)}, u32[]{:S(2)}, u32[]{:S(2)}) collective-permute-start(bf16[256,256]{1,0:T(8,128)(2,1)} %dynamic-slice_convert_fusion.6), channel_id=1, source_target_pairs={{0,16},{4,20},{8,24},{12,28},{16,0},{20,4},{24,8},{28,12},{1,17},{... | collective-permute-start | bytes 393224 | tf_op jit(solution)/shard_map/ppermute | solution.py:442
  162.0 1.3 copy-start.2
  163.3 24.1 %copy-start.16 = (bf16[256,1024]{1,0:T(8,128)(2,1)S(1)}, bf16[256,1024]{1,0:T(8,128)(2,1)}, u32[]{:S(2)}) copy-start(bf16[256,1024]{1,0:T(8,128)(2,1)} %param.13) | copy-start | bytes 1572868
  176.5 13.3 %copy-start.29 = (f32[512,256]{1,0:T(8,128)S(1)}, f32[512,256]{1,0:T(8,128)}, u32[]{:S(2)}) copy-start(f32[512,256]{1,0:T(8,128)} %copy-done.28) | copy-start | bytes 1572868
  176.5 13.3 %copy-start.9 = (bf16[256,1024]{1,0:T(8,128)(2,1)S(1)}, bf16[256,1024]{1,0:T(8,128)(2,1)}, u32[]{:S(2)}) copy-start(bf16[256,1024]{1,0:T(8,128)(2,1)} %copy-done.8) | copy-start | bytes 1572868
  176.5 13.3 %copy-start.24 = (bf16[256,512]{1,0:T(8,128)(2,1)S(1)}, bf16[256,512]{1,0:T(8,128)(2,1)}, u32[]{:S(2)}) copy-start(bf16[256,512]{1,0:T(8,128)(2,1)} %copy-done.23) | copy-start | bytes 786436
  189.8 7.0 %copy-start.32 = (f32[256,256]{1,0:T(8,128)}, f32[256,256]{1,0:T(8,128)S(1)}, u32[]{:S(2)}) copy-start(f32[256,256]{1,0:T(8,128)S(1)} %convert_add_fusion.10) | copy-start | bytes 786436
  189.8 3.7 %copy-start.14 = (f32[512,1408]{1,0:T(8,128)S(1)}, f32[512,1408]{1,0:T(8,128)}, u32[]{:S(2)}) copy-start(f32[512,1408]{1,0:T(8,128)} %copy-done.13) | copy-start | bytes 8650756
  191.5 1.2 copy-start.18
  193.5 3.2 %copy-start.44 = (f32[1024]{0:T(1024)S(1)}, f32[1024]{0:T(1024)}, u32[]{:S(2)}) copy-start(f32[1024]{0:T(1024)} %get-tuple-element.107) | copy-start | bytes 12292
  193.5 3.2 %copy-start.36 = (f32[7168]{0:T(1024)S(1)}, f32[7168]{0:T(1024)}, u32[]{:S(2)}) copy-start(f32[7168]{0:T(1024)} %pad.35.clone) | copy-start | bytes 86020
  194.8 1.1 copy-start.22
  195.9 6.6 %copy-start.51 = (f32[256]{0:T(256)S(1)}, f32[256]{0:T(256)}, u32[]{:S(2)}) copy-start(f32[256]{0:T(256)} %copy-done.50) | copy-start | bytes 3076
  195.9 7.2 %copy-start.5 = (bf16[256,1024]{1,0:T(8,128)(2,1)S(1)}, bf16[256,1024]{1,0:T(8,128)(2,1)}, u32[]{:S(2)}) copy-start(bf16[256,1024]{1,0:T(8,128)(2,1)} %x_ref.1) | copy-start | bytes 1572868
  195.9 7.2 %copy-start.47 = (f32[256]{0:T(256)S(1)}, f32[256]{0:T(256)}, u32[]{:S(2)}) copy-start(f32[256]{0:T(256)} %copy-done.46) | copy-start | bytes 3076
  197.6 44.6 %collective-permute-start.9 = (bf16[256,768]{1,0:T(8,128)(2,1)}, bf16[256,768]{1,0:T(8,128)(2,1)}, u32[]{:S(2)}, u32[]{:S(2)}) collective-permute-start(bf16[256,768]{1,0:T(8,128)(2,1)} %dynamic-slice_convert_fusion.1), channel_id=1, source_target_pairs={{0,16},{4,20},{8,24},{12,28},{16,0},{20,4},{24,8},{28,12},{1,17},{... | collective-permute-start | bytes 1179656 | tf_op jit(solution)/shard_map/ppermute | solution.py:442
  200.1 37.2 %collective-permute-start.11 = (bf16[128,256]{1,0:T(8,128)(2,1)S(1)}, bf16[128,256]{1,0:T(8,128)(2,1)S(1)}, u32[]{:S(2)}, u32[]{:S(2)}) collective-permute-start(bf16[128,256]{1,0:T(8,128)(2,1)S(1)} %dynamic-slice_convert_fusion.7), channel_id=1, source_target_pairs={{0,4},{4,0},{8,12},{12,8},{16,20},{20,16},{24,28},{28,24},{1,5},{5... | collective-permute-start | bytes 196616 | tf_op jit(solution)/shard_map/ppermute | solution.py:442
  201.7 38.4 %collective-permute-start.12 = (bf16[128,1408]{1,0:T(8,128)(2,1)}, bf16[128,1408]{1,0:T(8,128)(2,1)}, u32[]{:S(2)}, u32[]{:S(2)}) collective-permute-start(bf16[128,1408]{1,0:T(8,128)(2,1)} %dynamic-slice_convert_fusion.2), channel_id=1, source_target_pairs={{0,16},{4,20},{8,24},{12,28},{16,0},{20,4},{24,8},{28,12},{1,17},{... | collective-permute-start | bytes 1081352 | tf_op jit(solution)/shard_map/ppermute | solution.py:442
  202.1 36.0 %collective-permute-start.13 = (bf16[128,704]{0,1:T(8,128)(2,1)}, bf16[128,704]{0,1:T(8,128)(2,1)}, u32[]{:S(2)}, u32[]{:S(2)}) collective-permute-start(bf16[128,704]{0,1:T(8,128)(2,1)} %dynamic-slice_convert_fusion.5), channel_id=1, source_target_pairs={{0,4},{4,0},{8,12},{12,8},{16,20},{20,16},{24,28},{28,24},{1,5},{5... | collective-permute-start | bytes 540680 | tf_op jit(solution)/shard_map/ppermute | solution.py:442
  203.1 3.8 %copy-start.10 = (f32[1,8,56,128]{3,2,1,0:T(8,128)S(1)}, f32[1,8,56,128]{3,2,1,0:T(8,128)}, u32[]{:S(2)}) copy-start(f32[1,8,56,128]{3,2,1,0:T(8,128)} %copy.46) | copy-start | bytes 688132
  203.1 34.2 %copy-start.33 = (f32[256,256]{1,0:T(8,128)S(1)}, f32[256,256]{1,0:T(8,128)}, u32[]{:S(2)}) copy-start(f32[256,256]{1,0:T(8,128)} %copy-done.32) | copy-start | bytes 786436
  238.1 5.2 %copy-start.19 = (f32[512,768]{1,0:T(8,128)S(1)}, f32[512,768]{1,0:T(8,128)}, u32[]{:S(2)}) copy-start(f32[512,768]{1,0:T(8,128)} %copy-done.18) | copy-start | bytes 4718596
  245.3 5.7 %collective-permute-start.10 = (bf16[128,768]{1,0:T(8,128)(2,1)S(1)}, bf16[128,768]{1,0:T(8,128)(2,1)S(1)}, u32[]{:S(2)}, u32[]{:S(2)}) collective-permute-start(bf16[128,768]{1,0:T(8,128)(2,1)S(1)} %dynamic-slice_convert_fusion.4), channel_id=1, source_target_pairs={{0,4},{4,0},{8,12},{12,8},{16,20},{20,16},{24,28},{28,24},{1,5},{5... | collective-permute-start | bytes 589832 | tf_op jit(solution)/shard_map/ppermute | solution.py:442
  (9 other events, 6.6 us)
Sparse Core Ops, SparseCore 0:
  155.3 36.2 all-reduce.8
